TPU v7x, 128 devices: a whole 4x4x4 slice. The times are simulated.
128 devices in a mesh: depth: 4 (over y_hi, core), row: 4 (over z), col: 8 (over x, y_lo).
Axes of the slice: x: 4, y: 4 (y_hi: 2, y_lo: 2; y = y_hi * 2 + y_lo), z: 4, core: 2. Of those that a mesh axis runs over, the one named last changes fastest.
Arguments:
- left_factor: bfloat16 [1792, 32, 512], P('depth', None, 'row'), may hold values from -6 to 6
- right_factor: bfloat16 [1792, 32, 512], P('depth', None, 'col'), may hold values from -6 to 6
- out_weight: bfloat16 [1024, 128], replicated, may hold values from -12 to 12
- pair_cotangent: bfloat16 [512, 512, 128], P(('row', 'depth'), 'col'), may hold values from -0.29882812 to 0.29882812
Outputs:
- left_grad: float32 [1792, 32, 512], P(('depth', 'col'), None, 'row')
- right_grad: float32 [1792, 32, 512], P(('depth', 'row'), None, 'col')
- weight_grad: float32 [1024, 128], P(('depth', 'row', 'col'))
All inputs are finite; a program needn't handle non-finite values.
Results may differ from a plain program's by a relative error of at most 0.0075.
Values may be sent and summed in bfloat16 or wider, within the bound.
No kernel may reach another device: no remote copies, remote signals or barrier semaphores. Data moves between devices by JAX's collectives and lax.ppermute only.
A program may use at most 256 MiB of HBM per device.

v0:
```python
import jax
import jax.numpy as jnp
from jax import lax
from jax.sharding import Mesh
from jax.sharding import PartitionSpec as P

COL = ("col_0", "col_1")
DEPTH_COL = ("depth", "col_0", "col_1")
DEPTH_ROW_COL = ("depth", "row", "col_0", "col_1")


def laid_out(blocks, dim):
    dims = list(blocks.shape[1:])
    dims[dim] *= blocks.shape[0]
    return jnp.moveaxis(blocks, 0, dim).reshape(dims)


def copy_for_each(array, axis):
    copies = jnp.broadcast_to(array, (lax.axis_size(axis), *array.shape))
    return lax.all_to_all(copies, axis, split_axis=0, concat_axis=0, tiled=True)


def gather_directly(array, axis, dim):
    return laid_out(copy_for_each(array, axis), dim)


def split_up(array, dim, peers):
    before, after = (array.shape[:dim], array.shape[dim + 1 :])
    return jnp.moveaxis(array.reshape(*before, peers, -1, *after), dim, 0)


def summed_on_arrival(array, axis, dim):
    peers = lax.axis_size(axis)
    blocks = lax.all_to_all(split_up(array, dim, peers), axis, 0, 0, tiled=True)
    return jnp.sum(blocks, axis=0)


def sum_by_axis(array, axes, dim):
    for axis in axes:
        array = lax.psum_scatter(array, axis, scatter_dimension=dim, tiled=True)
    return array


def body(left_factor, right_factor, out_weight, pair_cotangent):
    seq_total = left_factor.shape[0] * lax.axis_size("depth")
    chans = left_factor.shape[1]
    rows_here = left_factor.shape[2]
    cols_here = right_factor.shape[2]
    width = out_weight.shape[0]
    pair_ch = out_weight.shape[1]
    natural = (
        jnp.einsum("sci,sej->ciej", left_factor, right_factor, preferred_element_type=jnp.float32)
        / seq_total
    )
    natural = natural.astype(jnp.bfloat16)
    outer = jnp.transpose(natural, (1, 3, 0, 2)).reshape(rows_here, cols_here, width)
    piece = gather_directly(pair_cotangent, "depth", 0)
    count = piece.shape[0]
    grad_two = piece.reshape(count * cols_here, pair_ch)
    fresh = jnp.dot(grad_two, out_weight.T, preferred_element_type=jnp.float32).astype(jnp.bfloat16)
    delta_acc = fresh.reshape(count, cols_here, width)
    outer_rows = outer.reshape(count * cols_here, width)
    weight_acc = jnp.dot(outer_rows.T, grad_two, preferred_element_type=jnp.float32)
    delta_four = delta_acc.reshape(rows_here, cols_here, chans, chans)
    left_part = (
        jnp.einsum("ijce,sej->sci", delta_four, right_factor, preferred_element_type=jnp.float32)
        / seq_total
    )
    right_part = (
        jnp.einsum("ijce,sci->sej", delta_four, left_factor, preferred_element_type=jnp.float32)
        / seq_total
    )
    left_grad = sum_by_axis(left_part, COL, 0)
    right_grad = summed_on_arrival(right_part, "row", 0)
    middle = summed_on_arrival(weight_acc, ("depth", "row"), 0)
    weight_grad = summed_on_arrival(middle, COL, 0)
    return (left_grad, right_grad, weight_grad)


def solution(mesh):
    finer = Mesh(
        mesh.devices.reshape(mesh.shape["depth"], mesh.shape["row"], 4, 2),
        ("depth", "row", "col_0", "col_1"),
    )
    in_specs = (P("depth", None, "row"), P("depth", None, COL), P(), P(("row", "depth"), COL, None))
    out_specs = (P(DEPTH_COL, None, "row"), P(("depth", "row"), None, COL), P(DEPTH_ROW_COL, None))
    return jax.shard_map(body, mesh=finer, in_specs=in_specs, out_specs=out_specs, check_vma=False)
```

profile of v0, /device:TPU:0, one launch (start us, length us, event | category | flops | bytes accessed | tf_op | source)
XLA Modules:
  0.0 365.2 jit_solution(12715900445172203453)
XLA Ops:
  7.2 0.0 reduce-scatter.3.cloned.1.call-start
  7.2 1.7 broadcast_in_dim.3
  9.0 31.7 %all_to_all.20 = bf16[4,32,64,128]{3,2,1,0:T(8,128)(2,1)} all-to-all(bf16[4,32,64,128]{3,2,1,0:T(8,128)(2,1)S(1)} %broadcast_in_dim.3), channel_id=1, replica_groups=mesh['depth'=4,'row'=4,'col_0'=4,'col_1'=2] {'depth'}, dimensions={0} | all-to-all | bytes 4194304 | tf_op jit(solution)/shard_map/all_to_all | solution.py:20
  40.6 9.8 %convolution_convert_fusion = bf16[8192,1024]{1,0:T(8,128)(2,1)} fusion(bf16[8192,128]{1,0:T(8,128)(2,1)} %bitcast.44, bf16[1024,128]{1,0:T(8,128)(2,1)S(1)} %copy-done.3), kind=kOutput, calls=%fused_computation.2 | convolution fusion | flops 2155872256 | bytes 19136512 | tf_op jit(solution)/shard_map/dot_general | solution.py:60
  50.5 20.7 %copy.29 = bf16[8192,1024]{0,1:T(8,128)(2,1)} copy(bf16[8192,1024]{1,0:T(8,128)(2,1)} %convolution_convert_fusion) | data formatting | bytes 33554432 | tf_op jit(solution)/shard_map/convert_element_type | solution.py:60
  71.2 46.0 %reshape_reshape.10 = bf16[128,64,32,32]{1,0,3,2:T(8,128)(2,1)} reshape(bf16[8192,1024]{0,1:T(8,128)(2,1)} %copy.29) | data formatting | bytes 33554432 | tf_op jit(solution)/shard_map/reshape;reshape | solution.py:64
  117.2 20.7 %fusion.1 = f32[448,32,128]{2,0,1:T(8,128)} fusion(bf16[128,64,32,32]{1,0,3,2:T(8,128)(2,1)} %reshape_reshape.10, bf16[448,32,64]{0,2,1:T(8,128)(2,1)S(1)} %copy-done), kind=kOutput, calls=%fused_computation.4 | convolution fusion | flops 7518027776 | bytes 25952256 | tf_op jit(solution)/shard_map/ijce,sej->sci/dot_general | solution.py:66
  137.9 15.4 %fusion = bf16[128,64,32,32]{0,1,3,2:T(8,128)(2,1)} fusion(bf16[448,32,128,1]{2,1,0,3:T(8,128)(2,1)} %bitcast.46, bf16[448,32,64]{0,2,1:T(8,128)(2,1)S(1)} %copy-done), kind=kOutput, calls=%fused_computation.1 | convolution fusion | flops 7532969984 | bytes 22282240 | tf_op jit(solution)/shard_map/sci,sej->ciej/dot_general | solution.py:52
  153.3 30.1 %copy.36 = bf16[128,64,32,32]{1,0,3,2:T(8,128)(2,1)} copy(bf16[128,64,32,32]{0,1,3,2:T(8,128)(2,1)} %fusion) | data formatting | bytes 33554432 | tf_op jit(solution)/shard_map/convert_element_type | solution.py:55
  183.4 44.3 %reshape_reshape.11 = bf16[8192,1024]{0,1:T(8,128)(2,1)} reshape(bf16[128,64,32,32]{1,0,3,2:T(8,128)(2,1)} %copy.36) | data formatting | bytes 33554432 | tf_op jit(solution)/shard_map/reshape;reshape | solution.py:62
  227.7 8.1 %fusion.10 = f32[16,64,128]{2,1,0:T(8,128)S(1)} fusion(bf16[16,64,8192]{2,1,0:T(8,128)(2,1)} %bitcast.43, bf16[8192,128,1]{1,0,2:T(8,128)(2,1)S(1)} %bitcast.45), kind=kOutput, calls=%fused_computation.12 | convolution fusion | flops 2147483648 | bytes 19398656 | tf_op jit(solution)/shard_map/dot_general | solution.py:63
  235.8 17.5 %all_to_all.21 = f32[16,64,128]{2,1,0:T(8,128)S(1)} all-to-all(f32[16,64,128]{2,1,0:T(8,128)S(1)} %fusion.10), channel_id=1, replica_groups=mesh['depth'=4,'row'=4,'col_0'=4,'col_1'=2] {'depth','row'}, dimensions={0} | all-to-all | bytes 1048576 | tf_op jit(solution)/shard_map/all_to_all | solution.py:34
  253.3 0.6 reduce_sum.28
  254.0 4.4 %all-to-all-start.3 = ((f32[8,8,128]{2,1,0:T(8,128)}), f32[8,8,128]{2,1,0:T(8,128)S(1)}, u32[]{:S(2)}, u32[]{:S(2)}) async-start(f32[8,8,128]{2,1,0:T(8,128)} %bitcast.13), calls=%async_computation.5 | async-start | bytes 65536 | tf_op jit(solution)/shard_map/all_to_all | solution.py:34
  258.5 0.7 reduce-scatter.5.cloned.1.call-update
  259.1 26.2 %fusion.2 = f32[448,32,64]{0,2,1:T(8,128)} fusion(bf16[128,64,32,32]{1,0,3,2:T(8,128)(2,1)} %reshape_reshape.10, bf16[448,32,128,1]{2,1,0,3:T(8,128)(2,1)} %bitcast.47), kind=kOutput, calls=%fused_computation.6 | convolution fusion | flops 7517110272 | bytes 24117248 | tf_op jit(solution)/shard_map/ijce,sci->sej/dot_general | solution.py:70
  285.3 5.9 %reshape.14 = f32[4,112,32,64]{1,0,3,2:T(4,128)} reshape(f32[448,32,64]{0,2,1:T(8,128)} %fusion.2) | data formatting | bytes 7340032 | tf_op jit(solution)/shard_map/reshape | solution.py:29
  291.2 6.6 %copy.33 = f32[4,112,32,64]{1,2,3,0:T(8,128)} copy(f32[4,112,32,64]{1,0,3,2:T(4,128)} %reshape.14) | data formatting | bytes 7340032 | tf_op jit(solution)/shard_map/reshape | solution.py:29
  297.8 4.9 %all-to-all-start.1 = ((f32[4,112,32,64]{1,2,3,0:T(8,128)}), f32[4,112,32,64]{1,2,3,0:T(8,128)}, u32[]{:S(2)}, u32[]{:S(2)}) async-start(f32[4,112,32,64]{1,2,3,0:T(8,128)} %copy.33), calls=%async_computation.3 | async-start | bytes 8388608 | tf_op jit(solution)/shard_map/all_to_all | solution.py:34
  302.7 0.6 reduce_sum.29
  303.3 48.4 %all-to-all-done.1 = f32[4,112,32,64]{1,2,3,0:T(8,128)} async-done(((f32[4,112,32,64]{1,2,3,0:T(8,128)}), f32[4,112,32,64]{1,2,3,0:T(8,128)}, u32[]{:S(2)}, u32[]{:S(2)}) %all-to-all-start.1) | async-done | bytes 3670048 | tf_op jit(solution)/shard_map/all_to_all | solution.py:34
  351.7 2.8 reduce_sum.27
  354.5 1.6 copy.38
  356.1 2.3 copy.37
  (13 shorter events, 0.1 us)
Async XLA Ops:
  7.2 110.0 %copy-start = (bf16[448,32,64]{0,2,1:T(8,128)(2,1)S(1)}, bf16[448,32,64]{0,2,1:T(8,128)(2,1)}, u32[]{:S(2)}) copy-start(bf16[448,32,64]{0,2,1:T(8,128)(2,1)} %param.5) | copy-start | bytes 5505028
  7.2 33.4 %copy-start.3 = (bf16[1024,128]{1,0:T(8,128)(2,1)S(1)}, bf16[1024,128]{1,0:T(8,128)(2,1)}, u32[]{:S(2)}) copy-start(bf16[1024,128]{1,0:T(8,128)(2,1)} %param.6) | copy-start | bytes 786436
  7.2 251.3 %reduce-scatter.3.cloned.1.call-start = ((), (), s32[]{:S(2)}) async-start(), calls=%async_computation.6 | async-start | bytes 9175040 | tf_op jit(solution)/shard_map/reduce_scatter | solution.py:40
  183.4 44.3 %copy-start.2 = (bf16[4,32,64,128]{3,2,1,0:T(8,128)(2,1)S(1)}, bf16[4,32,64,128]{3,2,1,0:T(8,128)(2,1)}, u32[]{:S(2)}) copy-start(bf16[4,32,64,128]{3,2,1,0:T(8,128)(2,1)} %all_to_all.20) | copy-start | bytes 6291460
  254.0 43.9 %all-to-all-start.3 = ((f32[8,8,128]{2,1,0:T(8,128)}), f32[8,8,128]{2,1,0:T(8,128)S(1)}, u32[]{:S(2)}, u32[]{:S(2)}) async-start(f32[8,8,128]{2,1,0:T(8,128)} %bitcast.13), calls=%async_computation.5 | async-start | bytes 65536 | tf_op jit(solution)/shard_map/all_to_all | solution.py:34
  258.4 97.7 %reduce-scatter.5.cloned.1.call-start = ((), (), s32[]{:S(2)}) async-start(), calls=%async_computation.7 | async-start | bytes 2752512 | tf_op jit(solution)/shard_map/reduce_scatter | solution.py:40
  297.8 53.9 %all-to-all-start.1 = ((f32[4,112,32,64]{1,2,3,0:T(8,128)}), f32[4,112,32,64]{1,2,3,0:T(8,128)}, u32[]{:S(2)}, u32[]{:S(2)}) async-start(f32[4,112,32,64]{1,2,3,0:T(8,128)} %copy.33), calls=%async_computation.3 | async-start | bytes 8388608 | tf_op jit(solution)/shard_map/all_to_all | solution.py:34
  302.7 55.7 %copy-start.1 = (bf16[448,32,64]{0,2,1:T(8,128)(2,1)S(1)}, bf16[448,32,64]{0,2,1:T(8,128)(2,1)}, u32[]{:S(2)}) copy-start(bf16[448,32,64]{0,2,1:T(8,128)(2,1)} %param.5) | copy-start | bytes 5505028
Sparse Core Ops, SparseCore 0:
  138.1 72.3 reduce-scatter.2
  261.6 29.9 reduce-scatter.4
where the time goes:
time: 370 us; the launch traced here: 365 us
  local copies, waits for them, and re-layouts  159 us (43%)
  matrix products  80.3 us (22%)
  blocking collectives  49.1 us (13%)
  waiting for transfers between devices  49.1 us (13%)
  between operations  14.1 us (4%)
  starting transfers between devices  9.36 us (3%)
  other arithmetic  4.09 us (1%)
    all_to_all x2, waiting for transfers between devices, summed_on_arrival(): blocks = lax.all_to_all(split_up(array, dim, peers), axis, 0, 0, tiled=True)  48.4 us
    another operation x1, local copies, waits for them, and re-layouts, body(): delta_four = delta_acc.reshape(rows_here, cols_here, chans, chans)  46 us
    another operation x1, local copies, waits for them, and re-layouts, body(): outer_rows = outer.reshape(count * cols_here, width)  44.3 us
    all_to_all x1, blocking collectives, copy_for_each(): return lax.all_to_all(copies, axis, split_axis=0, concat_axis=0, tiled=True)  31.7 us
    convert_element_type x1, local copies, waits for them, and re-layouts, body(): natural = natural.astype(jnp.bfloat16)  30.1 us
    dot_general x1, matrix products, body(): jnp.einsum('ijce,sci->sej', delta_four, left_factor, preferred_element_ty...  26.2 us
    dot_general x1, matrix products, body(): jnp.einsum('ijce,sej->sci', delta_four, right_factor, preferred_element_t...  20.7 us
    convert_element_type x1, local copies, waits for them, and re-layouts, body(): jnp.dot(grad_two, out_weight.T, preferred_element_type=jnp.float32)  20.7 us
  transfers between devices with their start and end apart: 4, of which 1 were waited for; matrix products, arithmetic and copies ran while one was open for 39% of the time, Pallas kernels for 0%

commit v1 on v0

v1 whole, which is shorter than its diff:
```python
import functools

import jax
import jax.numpy as jnp
from jax import lax
from jax.experimental import pallas as pl
from jax.experimental.pallas import tpu as pltpu
from jax.sharding import Mesh
from jax.sharding import PartitionSpec as P

BF16 = jnp.bfloat16
F32 = jnp.float32
COL = ("x", "yl")
DEPTH = ("yh", "core")
EVERY = ("yh", "core", "row", "x", "yl")
NT = (((1,), (1,)), ((), ()))
VMEM_LIMIT = 56 * 1024 * 1024


def vmem_spec():
    return pl.BlockSpec(memory_space=pltpu.VMEM)


def params():
    return pltpu.CompilerParams(vmem_limit_bytes=VMEM_LIMIT)


def cost(flops, moved):
    return pl.CostEstimate(flops=flops, bytes_accessed=moved, transcendentals=0)


def outer_kernel(bt_ref, a_ref, out_ref):
    out_ref[...] = jnp.dot(bt_ref[...], a_ref[...], preferred_element_type=F32).astype(BF16)


def outer_call(bt, ap):
    m, k = bt.shape
    n = ap.shape[1]
    tile = 512
    return pl.pallas_call(
        outer_kernel,
        grid=(n // tile,),
        in_specs=[pl.BlockSpec((m, k), lambda g: (0, 0)), pl.BlockSpec((k, tile), lambda g: (0, g))],
        out_specs=pl.BlockSpec((m, tile), lambda g: (0, g)),
        out_shape=jax.ShapeDtypeStruct((m, n), BF16),
        compiler_params=params(),
        cost_estimate=cost(2 * m * n * k, 2 * (m * n + m * k + k * n)),
        name="outer",
    )(bt, ap)


def place_pieces(me_ref, pieces, pairs_ref):
    rows = pieces[0].shape[1]
    for step, piece in enumerate(pieces):
        at = pl.multiple_of(jnp.bitwise_xor(me_ref[0], step) * rows, rows)
        pairs_ref[:, pl.ds(at, rows), :] = piece[...]


def left_kernel(chans, me_ref, g0, g1, g2, g3, w_ref, bp_ref, delta_ref, left_ref, pairs_ref):
    width = pairs_ref.shape[1]

    @pl.when(pl.program_id(0) == 0)
    def _():
        place_pieces(me_ref, (g0, g1, g2, g3), pairs_ref)

    here = w_ref.shape[0] // chans

    def step(t, carry):
        g = pairs_ref[pl.ds(2 * t, 2)].reshape(2 * width, -1)
        d = lax.dot_general(w_ref[...], g, NT, preferred_element_type=F32).astype(BF16)
        for u in range(2):
            rows = pl.ds(pl.multiple_of((2 * t + u) * chans, chans), chans)
            for c in range(here):
                delta_ref[rows, c * width : (c + 1) * width] = d[
                    c * chans : (c + 1) * chans, u * width : (u + 1) * width
                ]
        return carry

    lax.fori_loop(0, pairs_ref.shape[0] // 2, step, 0, unroll=4)
    left_ref[...] = jnp.dot(bp_ref[...], delta_ref[...], preferred_element_type=F32).astype(BF16)


def left_call(me, pieces, w, bp, chans):
    cols, rows, pair = pieces[0].shape
    width = 4 * rows
    seqs, k = bp.shape
    n = chans * width
    steps = 4
    tile = n // steps
    whole = pl.BlockSpec((cols, rows, pair), lambda g: (0, 0, 0))
    return pl.pallas_call(
        functools.partial(left_kernel, chans),
        grid=(steps,),
        in_specs=[
            pl.BlockSpec(memory_space=pltpu.SMEM),
            whole,
            whole,
            whole,
            whole,
            pl.BlockSpec((w.shape[0] // steps, pair), lambda g: (g, 0)),
            pl.BlockSpec((seqs, k), lambda g: (0, 0)),
        ],
        out_specs=[pl.BlockSpec((k, tile), lambda g: (0, g)), pl.BlockSpec((seqs, tile), lambda g: (0, g))],
        out_shape=[jax.ShapeDtypeStruct((k, n), BF16), jax.ShapeDtypeStruct((seqs, n), BF16)],
        scratch_shapes=[pltpu.VMEM((cols, width, pair), BF16)],
        compiler_params=params(),
        cost_estimate=cost(2 * k * n * (pair * 2 + seqs), 2 * (k * n + seqs * n + seqs * k)),
        name="left",
    )(me, *pieces, w, bp)


def right_kernel(a_ref, delta_ref, out_ref, acc_ref):
    g = pl.program_id(0)
    part = lax.dot_general(a_ref[...], delta_ref[...], NT, preferred_element_type=F32)

    @pl.when(g == 0)
    def _():
        acc_ref[...] = part

    @pl.when(g > 0)
    def _():
        acc_ref[...] += part

    @pl.when(g == pl.num_programs(0) - 1)
    def _():
        out_ref[...] = acc_ref[...].astype(BF16)


def right_call(ap, delta):
    seqs, k = ap.shape
    n = delta.shape[0]
    tile = 1024
    return pl.pallas_call(
        right_kernel,
        grid=(k // tile,),
        in_specs=[pl.BlockSpec((seqs, tile), lambda g: (0, g)), pl.BlockSpec((n, tile), lambda g: (0, g))],
        out_specs=pl.BlockSpec((seqs, n), lambda g: (0, 0)),
        out_shape=jax.ShapeDtypeStruct((seqs, n), BF16),
        scratch_shapes=[pltpu.VMEM((seqs, n), F32)],
        compiler_params=params(),
        cost_estimate=cost(2 * k * n * seqs, 2 * (k * n + seqs * n + seqs * k)),
        name="right",
    )(ap, delta)


def weight_kernel(chans, me_ref, g0, g1, g2, g3, outer_ref, out_ref, pairs_ref, acc_ref):
    step = pl.program_id(0)
    width = pairs_ref.shape[1]

    @pl.when(step == 0)
    def _():
        place_pieces(me_ref, (g0, g1, g2, g3), pairs_ref)
        acc_ref[...] = jnp.zeros_like(acc_ref)

    here = outer_ref.shape[0] // chans
    parts = []
    for u in range(here):
        rows = outer_ref[u * chans : (u + 1) * chans, :]
        parts.append(jnp.concatenate([rows[:, c * width : (c + 1) * width] for c in range(chans)], axis=0))
    g = pairs_ref[pl.ds(step * here, here)].reshape(here * width, -1)
    acc_ref[...] += jnp.dot(jnp.concatenate(parts, axis=1), g, preferred_element_type=F32)

    @pl.when(step == pl.num_programs(0) - 1)
    def _():
        out_ref[...] = acc_ref[...].astype(BF16)


def weight_call(me, pieces, outer, chans):
    cols, rows, pair = pieces[0].shape
    width = 4 * rows
    k, n = outer.shape
    here = 8
    whole = pl.BlockSpec((cols, rows, pair), lambda g: (0, 0, 0))
    return pl.pallas_call(
        functools.partial(weight_kernel, chans),
        grid=(cols // here,),
        in_specs=[
            pl.BlockSpec(memory_space=pltpu.SMEM),
            whole,
            whole,
            whole,
            whole,
            pl.BlockSpec((here * chans, n), lambda g: (g, 0)),
        ],
        out_specs=pl.BlockSpec((chans * chans, pair), lambda g: (0, 0)),
        out_shape=jax.ShapeDtypeStruct((chans * chans, pair), BF16),
        scratch_shapes=[pltpu.VMEM((cols, width, pair), BF16), pltpu.VMEM((chans * chans, pair), F32)],
        compiler_params=params(),
        cost_estimate=cost(4 * k * n * pair, 2 * k * n),
        name="weight",
    )(me, *pieces, outer)


def depth_exchange(array, other_chip, other_core):
    pairs = []
    for chip in range(2):
        for core in range(2):
            to = (chip ^ other_chip) * 2 + (core ^ other_core)
            pairs.append((chip * 2 + core, to))
    return lax.ppermute(array, DEPTH, pairs)


def summed(array, axes):
    peers = 1
    for axis in axes:
        peers *= lax.axis_size(axis)
    blocks = array.reshape(peers, array.shape[0] // peers, array.shape[1])
    blocks = lax.all_to_all(blocks, axes, 0, 0, tiled=True)
    return jnp.sum(blocks.astype(F32), axis=0)


def body(left_factor, right_factor, out_weight, pair_cotangent):
    seqs, chans, rows = left_factor.shape
    cols = right_factor.shape[2]
    scale = 1.0 / (seqs * lax.axis_size("yh") * lax.axis_size("core"))
    me = (lax.axis_index("yh") * 2 + lax.axis_index("core")).astype(jnp.int32).reshape(1)

    mine = jnp.transpose(pair_cotangent, (1, 0, 2))
    across = depth_exchange(mine, 1, 0)
    beside = depth_exchange(mine, 0, 1)
    both = depth_exchange(across, 0, 1)
    pieces = (mine, beside, across, both)

    ap = left_factor.reshape(seqs, chans * rows)
    bt = jnp.transpose(right_factor, (2, 1, 0)).reshape(cols * chans, seqs)
    bp = jnp.transpose(right_factor, (0, 2, 1)).reshape(seqs, cols * chans)

    outer = outer_call(bt, ap)
    delta, left_part = left_call(me, pieces, out_weight, bp, chans)
    right_part = right_call(ap, delta)
    weight_part = weight_call(me, pieces, outer, chans)

    left = summed(left_part, COL) * scale
    right = summed(right_part, ("row",)) * scale
    weight = summed(weight_part, EVERY) * scale
    left_grad = left.reshape(-1, chans, rows)
    right_grad = jnp.transpose(right.reshape(-1, cols, chans), (0, 2, 1))
    return left_grad, right_grad, weight


def solution(mesh):
    finer = Mesh(mesh.devices.reshape(2, 2, mesh.shape["row"], 4, 2), EVERY)
    in_specs = (P(DEPTH, None, "row"), P(DEPTH, None, COL), P(), P(("row",) + DEPTH, COL, None))
    out_specs = (P(DEPTH + COL, None, "row"), P(DEPTH + ("row",), None, COL), P(EVERY, None))
    return jax.shard_map(body, mesh=finer, in_specs=in_specs, out_specs=out_specs, check_vma=False)
```

time: 370 us -> 183 us (0.49)
  local copies, waits for them, and re-layouts: 159 us -> 20.2 us
  matrix products: 80.3 us -> 0 us
  Pallas kernels: 0 us -> 62.7 us
  blocking collectives: 49.1 us -> 27.8 us
  between operations: 14.1 us -> 0.71 us
  starting transfers between devices: 9.36 us -> 18.2 us
    another operation x2 -> x0, local copies, waits for them, and re-layouts: 90.3 us -> none  [the longest x1 46 us: body(): delta_four = delta_acc.reshape(rows_here, cols_here, chans, chans)]
    dot_general x5 -> x0, matrix products: 80.3 us -> none  [the longest x1 26.2 us: body(): jnp.einsum('ijce,sci->sej', delta_four, left_factor, preferred_element_ty...]
    pallas_call x0 -> x4, Pallas kernels: none -> 62.7 us  [the longest x1 23.3 us: left_call(): pl.pallas_call(functools.partial(left_kernel, chans), grid=(steps,), in_s...]
    convert_element_type x2 -> x0, local copies, waits for them, and re-layouts: 50.8 us -> none  [the longest x1 30.1 us: body(): natural = natural.astype(jnp.bfloat16)]
    all_to_all x2 -> x1, blocking collectives: 49.1 us -> 27.8 us  [summed(): blocks = lax.all_to_all(blocks, axes, 0, 0, tiled=True)]
    reshape x2 -> x1, local copies, waits for them, and re-layouts: 12.5 us -> 2.4 us  [body(): bp = jnp.transpose(right_factor, (0, 2, 1)).reshape(seqs, cols * chans)]
    unnamed x10 -> x12, local copies, waits for them, and re-layouts: 3.89 us -> 12.2 us
    transpose x0 -> x2, local copies, waits for them, and re-layouts: none -> 5.27 us  [the longest x1 2.75 us: body(): bp = jnp.transpose(right_factor, (0, 2, 1)).reshape(seqs, cols * chans)]
  transfers between devices with their start and end apart: 4 -> 5, of which waited for: 1 -> 1; matrix products, arithmetic and copies ran while one was open for 39% -> 10% of each run, Pallas kernels for 0% -> 28%
where the time goes in v1:
time: 183 us; the launch traced here: 182 us
  Pallas kernels  62.7 us (34%)
  waiting for transfers between devices  48.4 us (26%)
  blocking collectives  27.8 us (15%)
  local copies, waits for them, and re-layouts  20.2 us (11%)
  starting transfers between devices  18.2 us (10%)
  other arithmetic  3.94 us (2%)
    all_to_all x2, waiting for transfers between devices, summed(): blocks = lax.all_to_all(blocks, axes, 0, 0, tiled=True)  48.4 us
    all_to_all x1, blocking collectives, summed(): blocks = lax.all_to_all(blocks, axes, 0, 0, tiled=True)  27.8 us
    pallas_call x1, Pallas kernels, left_call(): pl.pallas_call(functools.partial(left_kernel, chans), grid=(steps,), in_s...  23.3 us
    all_to_all x2, starting transfers between devices, summed(): blocks = lax.all_to_all(blocks, axes, 0, 0, tiled=True)  14.3 us
    pallas_call x1, Pallas kernels, right_call(): pl.pallas_call(right_kernel, grid=(k // tile,), in_specs=[pl.BlockSpec((s...  13.7 us
    pallas_call x1, Pallas kernels, outer_call(): pl.pallas_call(outer_kernel, grid=(n // tile,), in_specs=[pl.BlockSpec((m...  13.7 us
    unnamed x12, local copies, waits for them, and re-layouts  12.2 us
    pallas_call x1, Pallas kernels, weight_call(): pl.pallas_call(functools.partial(weight_kernel, chans), grid=(cols // her...  11.9 us
  transfers between devices with their start and end apart: 5, of which 1 were waited for; matrix products, arithmetic and copies ran while one was open for 10% of the time, Pallas kernels for 28%

profile of v1, /device:TPU:0, one launch (start us, length us, event | category | flops | bytes accessed | tf_op | source)
XLA Modules:
  0.0 181.9 jit_solution(715350666149272635)
XLA Ops:
  0.6 1.4 copy.26
  2.0 3.4 %collective-permute-start.1 = (bf16[64,32,128]{2,1,0:T(8,128)(2,1)S(1)}, bf16[64,32,128]{2,1,0:T(8,128)(2,1)S(1)}, u32[]{:S(2)}, u32[]{:S(2)}) collective-permute-start(bf16[64,32,128]{2,1,0:T(8,128)(2,1)S(1)} %bitcast.29), channel_id=1, source_target_pairs={{0,64},{32,96},{64,0},{96,32},{1,65},{33,97},{65,1},{97,33},{2,66}... | collective-permute-start | bytes 1572872 | tf_op jit(solution)/shard_map/ppermute | solution.py:200
  5.4 2.8 %copy.16 = bf16[448,64,32]{0,2,1:T(8,128)(2,1)S(1)} copy(bf16[448,64,32]{0,1,2:T(8,128)(2,1)} %bitcast.21) | data formatting | bytes 3670016 | tf_op jit(solution)/shard_map/transpose | solution.py:226
  8.1 2.4 %copy.17.bp_ref = bf16[448,2048]{1,0:T(8,128)(2,1)} copy(bf16[448,2048]{0,1:T(8,128)(2,1)S(1)} %bitcast.23) | data formatting | bytes 3670016 | tf_op jit(solution)/shard_map/reshape | solution.py:226
  10.6 7.3 %copy.25 = bf16[56,8,32,128]{3,1,2,0:T(8,128)(2,1)} copy(bf16[56,8,32,128]{3,2,1,0:T(8,128)(2,1)} %bitcast.25) | data formatting | bytes 7340032
  17.9 2.5 %copy.19 = bf16[64,32,448]{2,1,0:T(8,128)(2,1)} copy(bf16[64,32,448]{2,0,1:T(8,128)(2,1)S(1)} %bitcast.22) | data formatting | bytes 3670016 | tf_op jit(solution)/shard_map/transpose | solution.py:225
  20.4 0.5 collective-permute-start.2
  20.9 13.7 %outer.1.outer_ref = bf16[2048,4096]{1,0:T(8,128)(2,1)} custom-call(bf16[2048,448]{1,0:T(8,128)(2,1)} %bitcast.33, bf16[448,4096]{1,0:T(8,128)(2,1)} %bitcast.26), custom_call_target="tpu_custom_call" | custom-call | flops 7516192768 | bytes 22282240 | tf_op jit(solution)/shard_map/outer/pallas_call | solution.py:40
  34.6 0.8 copy-done.3
  35.4 11.9 %weight.1 = bf16[1024,128]{1,0:T(8,128)(2,1)} custom-call(s32[1]{0:T(128)} %bitcast.me_ref, bf16[64,32,128]{2,1,0:T(8,128)(2,1)} %bitcast.31, bf16[64,32,128]{2,1,0:T(8,128)(2,1)} %collective-permute-done.g1, bf16[64,32,128]{2,1,0:T(8,128)(2,1)} %copy-done.2, bf16[64,32,128]{2,1,0:T(8,128)(2,1)} %copy-done.3, bf16[2048,4096]{1,0:T(8,128)(2,1)} %outer.1.outer_ref), custom_call_target="tpu_custom_call" | custom-call | flops 4294967296 | bytes 16777216 | tf_op jit(solution)/shard_map/weight/pallas_call | solution.py:174
  47.3 9.1 %all-to-all-start.2 = ((bf16[128,8,128]{2,1,0:T(8,128)(2,1)}), bf16[128,8,128]{2,1,0:T(8,128)(2,1)S(1)}, u32[]{:S(2)}, u32[]{:S(2)}) async-start(bf16[128,8,128]{2,1,0:T(8,128)(2,1)} %bitcast.35), calls=%async_computation.2 | async-start | bytes 524288 | tf_op jit(solution)/shard_map/all_to_all | solution.py:208
  56.4 23.3 %left.1 = (bf16[2048,4096]{1,0:T(8,128)(2,1)}, bf16[448,4096]{1,0:T(8,128)(2,1)}) custom-call(s32[1]{0:T(128)} %bitcast.me_ref, bf16[64,32,128]{2,1,0:T(8,128)(2,1)} %bitcast.32, bf16[64,32,128]{2,1,0:T(8,128)(2,1)} %collective-permute-done.g1, bf16[64,32,128]{2,1,0:T(8,128)(2,1)} %copy-done.2, bf16[64,32,128]{2,1,0:T(8,128)(2,1)} %copy-done.3, ...), custom_call_target="tpu_custom_call" | custom-call | flops 11811160064 | bytes 22282240 | tf_op jit(solution)/shard_map/left/pallas_call | solution.py:91
  79.8 13.7 %right.1 = bf16[448,2048]{1,0:T(8,128)(2,1)} custom-call(bf16[448,4096]{1,0:T(8,128)(2,1)} %bitcast.27, bf16[2048,4096]{1,0:T(8,128)(2,1)} %get-tuple-element.6.delta_ref), custom_call_target="tpu_custom_call" | custom-call | flops 7516192768 | bytes 22282240 | tf_op jit(solution)/shard_map/right/pallas_call | solution.py:133
  93.5 27.8 %all_to_all.15 = bf16[4,112,2048]{2,1,0:T(8,128)(2,1)S(1)} all-to-all(bf16[4,112,2048]{2,1,0:T(8,128)(2,1)} %bitcast.34), channel_id=1, replica_groups=mesh['yh'=2,'core'=2,'row'=4,'x'=4,'yl'=2] {'row'}, dimensions={0} | all-to-all | bytes 3670016 | tf_op jit(solution)/shard_map/all_to_all | solution.py:208
  121.2 5.2 %all-to-all-start = ((bf16[8,56,4096]{2,1,0:T(8,128)(2,1)}), bf16[8,56,4096]{2,1,0:T(8,128)(2,1)}, u32[]{:S(2)}, u32[]{:S(2)}) async-start(bf16[8,56,4096]{2,1,0:T(8,128)(2,1)} %bitcast.28), calls=%async_computation | async-start | bytes 7340032 | tf_op jit(solution)/shard_map/all_to_all | solution.py:208
  126.5 0.1 convert_reduce_fusion.2
  126.6 0.6 broadcast_multiply_fusion.1
  127.2 0.3 convert_reduce_fusion.1
  127.5 0.1 broadcast_multiply_fusion
  127.6 0.3 copy.18
  128.0 1.6 copy.20
  129.6 48.4 %all-to-all-done = bf16[8,56,4096]{2,1,0:T(8,128)(2,1)} async-done(((bf16[8,56,4096]{2,1,0:T(8,128)(2,1)}), bf16[8,56,4096]{2,1,0:T(8,128)(2,1)}, u32[]{:S(2)}, u32[]{:S(2)}) %all-to-all-start) | async-done | bytes 3670048 | tf_op jit(solution)/shard_map/all_to_all | solution.py:208
  178.0 2.7 %convert_reduce_fusion = f32[56,4096]{1,0:T(8,128)S(1)} fusion(bf16[8,56,4096]{2,1,0:T(8,128)(2,1)} %all-to-all-done), kind=kLoop, calls=%fused_computation | loop fusion | flops 3440640 | bytes 4587520 | tf_op jit(solution)/shard_map/reduce_sum | solution.py:209
  180.8 1.1 copy.21
  (13 shorter events, 0.1 us)
Async XLA Ops:
  2.0 8.5 %copy-start.1 = (bf16[32,64,128]{2,0,1:T(8,128)(2,1)}, bf16[32,64,128]{2,0,1:T(8,128)(2,1)S(1)}, u32[]{:S(2)}) copy-start(bf16[32,64,128]{2,0,1:T(8,128)(2,1)S(1)} %copy.26) | copy-start | bytes 1572868
  2.0 18.4 %collective-permute-start.1 = (bf16[64,32,128]{2,1,0:T(8,128)(2,1)S(1)}, bf16[64,32,128]{2,1,0:T(8,128)(2,1)S(1)}, u32[]{:S(2)}, u32[]{:S(2)}) collective-permute-start(bf16[64,32,128]{2,1,0:T(8,128)(2,1)S(1)} %bitcast.29), channel_id=1, source_target_pairs={{0,64},{32,96},{64,0},{96,32},{1,65},{33,97},{65,1},{97,33},{2,66}... | collective-permute-start | bytes 1572872 | tf_op jit(solution)/shard_map/ppermute | solution.py:200
  5.4 29.2 %collective-permute-start = (bf16[64,32,128]{2,1,0:T(8,128)(2,1)S(1)}, bf16[64,32,128]{2,1,0:T(8,128)(2,1)}, u32[]{:S(2)}, u32[]{:S(2)}) collective-permute-start(bf16[64,32,128]{2,1,0:T(8,128)(2,1)S(1)} %bitcast.30), channel_id=1, source_target_pairs={{0,32},{32,0},{64,96},{96,64},{1,33},{33,1},{65,97},{97,65},{2,34}... | collective-permute-start | bytes 1572872 | tf_op jit(solution)/shard_map/ppermute | solution.py:200
  10.6 7.3 %copy-start = (bf16[448,32,64]{0,2,1:T(8,128)(2,1)S(1)}, bf16[448,32,64]{0,2,1:T(8,128)(2,1)}, u32[]{:S(2)}) copy-start(bf16[448,32,64]{0,2,1:T(8,128)(2,1)} %param.5) | copy-start | bytes 5505028
  20.4 14.2 %copy-start.2 = (bf16[64,32,128]{2,1,0:T(8,128)(2,1)}, bf16[64,32,128]{2,1,0:T(8,128)(2,1)S(1)}, u32[]{:S(2)}) copy-start(bf16[64,32,128]{2,1,0:T(8,128)(2,1)S(1)} %collective-permute-done.1.g2) | copy-start | bytes 1572868
  20.4 14.2 %collective-permute-start.2 = (bf16[64,32,128]{2,1,0:T(8,128)(2,1)S(1)}, bf16[64,32,128]{2,1,0:T(8,128)(2,1)S(1)}, u32[]{:S(2)}, u32[]{:S(2)}) collective-permute-start(bf16[64,32,128]{2,1,0:T(8,128)(2,1)S(1)} %collective-permute-done.1.g2), channel_id=1, source_target_pairs={{0,32},{32,0},{64,96},{96,64},{1,33},{33,1},{65,97},{97,65},{2,34}... | collective-permute-start | bytes 1572872 | tf_op jit(solution)/shard_map/ppermute | solution.py:200
  34.6 0.8 copy-start.3
  47.3 46.1 %all-to-all-start.2 = ((bf16[128,8,128]{2,1,0:T(8,128)(2,1)}), bf16[128,8,128]{2,1,0:T(8,128)(2,1)S(1)}, u32[]{:S(2)}, u32[]{:S(2)}) async-start(bf16[128,8,128]{2,1,0:T(8,128)(2,1)} %bitcast.35), calls=%async_computation.2 | async-start | bytes 524288 | tf_op jit(solution)/shard_map/all_to_all | solution.py:208
  121.2 56.7 %all-to-all-start = ((bf16[8,56,4096]{2,1,0:T(8,128)(2,1)}), bf16[8,56,4096]{2,1,0:T(8,128)(2,1)}, u32[]{:S(2)}, u32[]{:S(2)}) async-start(bf16[8,56,4096]{2,1,0:T(8,128)(2,1)} %bitcast.28), calls=%async_computation | async-start | bytes 7340032 | tf_op jit(solution)/shard_map/all_to_all | solution.py:208

commit v2 on v1

v2 whole, which is shorter than its diff:
```python
import functools

import jax
import jax.numpy as jnp
from jax import lax
from jax.experimental import pallas as pl
from jax.experimental.pallas import tpu as pltpu
from jax.sharding import Mesh
from jax.sharding import PartitionSpec as P

BF16 = jnp.bfloat16
F32 = jnp.float32
COL = ("x", "yl")
DEPTH = ("yh", "core")
EVERY = ("yh", "core", "row", "x", "yl")
NT = (((1,), (1,)), ((), ()))
CHUNKS = 8
VMEM_LIMIT = 56 * 1024 * 1024


def params():
    return pltpu.CompilerParams(vmem_limit_bytes=VMEM_LIMIT)


def cost(flops, moved):
    return pl.CostEstimate(flops=flops, bytes_accessed=moved, transcendentals=0)


def place_pieces(me_ref, pieces, pairs_ref):
    rows = pieces[0].shape[1]
    for step, piece in enumerate(pieces):
        at = pl.multiple_of(jnp.bitwise_xor(me_ref[0], step) * rows, rows)
        pairs_ref[:, pl.ds(at, rows), :] = piece[...]


def left_kernel(
    chans, me_ref, from_ref, g0, g1, g2, g3, w_ref, bt_ref,
    delta_ref, keep_a, send_a, keep_b, send_b, pairs_ref, turned_ref, b_ref,
):
    grid_step = pl.program_id(0)
    width = pairs_ref.shape[1]
    rows = bt_ref.shape[1] // 4

    @pl.when(grid_step == 0)
    def _():
        place_pieces(me_ref, (g0, g1, g2, g3), pairs_ref)
        for k in range(0, bt_ref.shape[0], 128):
            turned_ref[:, k : k + 128] = bt_ref[k : k + 128, :].T
        for q in range(4):
            start = pl.multiple_of(from_ref[q] * rows, 16)
            b_ref[q * rows : (q + 1) * rows, :] = turned_ref[pl.ds(start, rows), :]

    here = w_ref.shape[0] // chans
    many = 16

    def step(t, carry):
        g = pairs_ref[pl.ds(many * t, many)].reshape(many * width, -1)
        d = lax.dot_general(w_ref[...], g, NT, preferred_element_type=F32).astype(BF16)
        for u in range(many):
            at = pl.ds(pl.multiple_of((many * t + u) * chans, chans), chans)
            for c in range(here):
                delta_ref[at, c * width : (c + 1) * width] = d[
                    c * chans : (c + 1) * chans, u * width : (u + 1) * width
                ]
        return carry

    lax.fori_loop(0, pairs_ref.shape[0] // many, step, 0, unroll=2)
    total = jnp.dot(b_ref[...], delta_ref[...], preferred_element_type=F32).astype(BF16)
    tile = keep_a.shape[2]
    count = total.shape[1] // tile

    @pl.when(grid_step < 2)
    def _():
        for q in range(count):
            at = grid_step * count + q
            cut = slice(q * tile, (q + 1) * tile)
            keep_a[at] = total[: 2 * rows, cut]
            send_a[at] = total[2 * rows :, cut]

    @pl.when(grid_step >= 2)
    def _():
        for q in range(count):
            at = (grid_step - 2) * count + q
            cut = slice(q * tile, (q + 1) * tile)
            for half in range(2):
                low = 2 * half * rows
                keep_b[at, half * rows : (half + 1) * rows] = total[low : low + rows, cut]
                send_b[at, half * rows : (half + 1) * rows] = total[low + rows : low + 2 * rows, cut]


def left_call(me, source, pieces, w, bt, chans):
    cols, rows, pair = pieces[0].shape
    width = 4 * rows
    k, seqs = bt.shape
    n = chans * width
    steps = 4
    tile = n // steps
    whole = pl.BlockSpec((cols, rows, pair), lambda g: (0, 0, 0))
    smem = pl.BlockSpec(memory_space=pltpu.SMEM)
    part = (CHUNKS // 2, seqs // 2, n // CHUNKS)
    return pl.pallas_call(
        functools.partial(left_kernel, chans),
        grid=(steps,),
        in_specs=[
            smem,
            smem,
            whole,
            whole,
            whole,
            whole,
            pl.BlockSpec((w.shape[0] // steps, pair), lambda g: (g, 0)),
            pl.BlockSpec((k, seqs), lambda g: (0, 0)),
        ],
        out_specs=[pl.BlockSpec((k, tile), lambda g: (0, g))] + [pl.BlockSpec(part, lambda g: (0, 0, 0))] * 4,
        out_shape=[jax.ShapeDtypeStruct((k, n), BF16)] + [jax.ShapeDtypeStruct(part, BF16)] * 4,
        scratch_shapes=[
            pltpu.VMEM((cols, width, pair), BF16),
            pltpu.VMEM((seqs, k), BF16),
            pltpu.VMEM((seqs, k), BF16),
        ],
        compiler_params=params(),
        cost_estimate=cost(2 * k * n * (pair * 2 + seqs), 2 * (k * n + seqs * n + seqs * k)),
        name="left",
    )(me, source, *pieces, w, bt)


def right_kernel(from_ref, a_ref, delta_ref, keep_a, send_a, keep_b, send_b, acc_ref):
    g = pl.program_id(0)
    rows = a_ref.shape[0] // 4
    a = jnp.concatenate(
        [a_ref[pl.ds(pl.multiple_of(from_ref[q] * rows, 16), rows), :] for q in range(4)], axis=0
    )
    part = lax.dot_general(a, delta_ref[...], NT, preferred_element_type=F32)

    @pl.when(g == 0)
    def _():
        acc_ref[...] = part

    @pl.when(g > 0)
    def _():
        acc_ref[...] += part

    @pl.when(g == pl.num_programs(0) - 1)
    def _():
        half = keep_a.shape[1]
        keep_a[...] = acc_ref[: 2 * rows, :half].astype(BF16)
        send_a[...] = acc_ref[2 * rows :, :half].astype(BF16)
        for q in range(2):
            low = 2 * q * rows
            to = slice(q * rows, (q + 1) * rows)
            keep_b[to] = acc_ref[low : low + rows, half:].astype(BF16)
            send_b[to] = acc_ref[low + rows : low + 2 * rows, half:].astype(BF16)


def right_call(source, ap, delta):
    seqs, k = ap.shape
    n = delta.shape[0]
    tile = 1024
    part = (seqs // 2, n // 2)
    return pl.pallas_call(
        right_kernel,
        grid=(k // tile,),
        in_specs=[
            pl.BlockSpec(memory_space=pltpu.SMEM),
            pl.BlockSpec((seqs, tile), lambda g: (0, g)),
            pl.BlockSpec((n, tile), lambda g: (0, g)),
        ],
        out_specs=[pl.BlockSpec(part, lambda g: (0, 0))] * 4,
        out_shape=[jax.ShapeDtypeStruct(part, BF16)] * 4,
        scratch_shapes=[pltpu.VMEM((seqs, n), F32)],
        compiler_params=params(),
        cost_estimate=cost(2 * k * n * seqs, 2 * (k * n + seqs * n + seqs * k)),
        name="right",
    )(source, ap, delta)


def left_end_kernel(scale, keep_ref, came_ref, out_ref):
    chunks, _, tile = keep_ref.shape
    width = out_ref.shape[2]
    per = tile // width
    for q in range(chunks):
        total = (keep_ref[q] + came_ref[q].astype(F32)) * scale
        for c in range(per):
            out_ref[:, q * per + c, :] = total[:, c * width : (c + 1) * width]


def left_end_call(keep, came, chans, scale):
    chunks, seqs, tile = keep.shape
    return pl.pallas_call(
        functools.partial(left_end_kernel, scale),
        out_shape=jax.ShapeDtypeStruct((seqs, chans, chunks * tile // chans), F32),
        compiler_params=params(),
        cost_estimate=cost(2 * keep.size, 10 * keep.size),
        name="left_end",
    )(keep, came)


def right_end_kernel(scale, keep_a, came_a, keep_b, came_b, out_ref, turned_ref):
    chans, cols, seqs = out_ref.shape
    half = keep_a.shape[1]
    for at, (keep, came) in enumerate(((keep_a, came_a), (keep_b, came_b))):
        for k in range(0, half, 128):
            total = (keep[:, k : k + 128].astype(F32) + came[:, k : k + 128].astype(F32)) * scale
            turned_ref[at * half + k : at * half + k + 128, :] = total.T
    for e in range(chans):
        out_ref[e] = turned_ref[pl.ds(e, cols, stride=chans), :]


def right_end_call(keep_a, came_a, keep_b, came_b, chans, scale):
    seqs, half = keep_a.shape
    cols = 2 * half // chans
    return pl.pallas_call(
        functools.partial(right_end_kernel, scale),
        out_shape=jax.ShapeDtypeStruct((chans, cols, seqs), F32),
        scratch_shapes=[pltpu.VMEM((2 * half, seqs), F32)],
        compiler_params=params(),
        cost_estimate=cost(4 * keep_a.size, 16 * keep_a.size),
        name="right_end",
    )(keep_a, came_a, keep_b, came_b)


def weight_kernel(chans, me_ref, g0, g1, g2, g3, bt_ref, a_ref, out_ref, pairs_ref, acc_ref):
    step = pl.program_id(0)
    width = pairs_ref.shape[1]

    @pl.when(step == 0)
    def _():
        place_pieces(me_ref, (g0, g1, g2, g3), pairs_ref)
        acc_ref[...] = jnp.zeros_like(acc_ref)

    here = bt_ref.shape[0] // chans
    g = pairs_ref[pl.ds(step * here, here)].reshape(here * width, -1)
    group = 8
    for q in range(chans // group):
        a = a_ref[:, q * group * width : (q + 1) * group * width]
        outer = jnp.dot(bt_ref[...], a, preferred_element_type=F32).astype(BF16)
        parts = []
        for u in range(here):
            rows = outer[u * chans : (u + 1) * chans]
            parts.append(jnp.concatenate([rows[:, c * width : (c + 1) * width] for c in range(group)], axis=0))
        acc_ref[q * group * chans : (q + 1) * group * chans, :] += jnp.dot(
            jnp.concatenate(parts, axis=1), g, preferred_element_type=F32
        )

    @pl.when(step == pl.num_programs(0) - 1)
    def _():
        out_ref[...] = acc_ref[...].astype(BF16)


def weight_call(me, pieces, bt, ap, chans):
    cols, rows, pair = pieces[0].shape
    width = 4 * rows
    k, seqs = bt.shape
    n = ap.shape[1]
    here = 16
    whole = pl.BlockSpec((cols, rows, pair), lambda g: (0, 0, 0))
    return pl.pallas_call(
        functools.partial(weight_kernel, chans),
        grid=(cols // here,),
        in_specs=[
            pl.BlockSpec(memory_space=pltpu.SMEM),
            whole,
            whole,
            whole,
            whole,
            pl.BlockSpec((here * chans, seqs), lambda g: (g, 0)),
            pl.BlockSpec((seqs, n), lambda g: (0, 0)),
        ],
        out_specs=pl.BlockSpec((chans * chans, pair), lambda g: (0, 0)),
        out_shape=jax.ShapeDtypeStruct((chans * chans, pair), BF16),
        scratch_shapes=[pltpu.VMEM((cols, width, pair), BF16), pltpu.VMEM((chans * chans, pair), F32)],
        compiler_params=params(),
        cost_estimate=cost(2 * k * n * (seqs + 2 * pair), 2 * (k * seqs + n * seqs)),
        name="weight",
    )(me, *pieces, bt, ap)


def depth_exchange(array, other_chip, other_core):
    pairs = []
    for chip in range(2):
        for core in range(2):
            to = (chip ^ other_chip) * 2 + (core ^ other_core)
            pairs.append((chip * 2 + core, to))
    return lax.ppermute(array, DEPTH, pairs)


def ring_partner(at, bit):
    return at ^ 1 if bit == 0 else 3 - at


def ring_place(at, bits):
    for bit in (0, 1):
        if bits[bit]:
            at = ring_partner(at, bit)
    return at


def ring_sources(at):
    here = [ring_place(at, (first, second)) for first in (0, 1) for second in (0, 1)]
    return jnp.stack(here).astype(jnp.int32)


def swap(array, axis, bit=None):
    if bit is None:
        pairs = [(0, 1), (1, 0)]
    else:
        pairs = [(at, ring_partner(at, bit)) for at in range(4)]
    return lax.ppermute(array, axis, pairs)


def join(keep, came, dtype=BF16):
    return (keep.astype(F32) + came.astype(F32)).astype(dtype)


def summed(array, axes):
    peers = 1
    for axis in axes:
        peers *= lax.axis_size(axis)
    blocks = array.reshape(peers, array.shape[0] // peers, array.shape[1])
    blocks = lax.all_to_all(blocks, axes, 0, 0, tiled=True)
    return jnp.sum(blocks.astype(F32), axis=0)


def body(left_factor, right_factor, out_weight, pair_cotangent):
    seqs, chans, rows = left_factor.shape
    cols = right_factor.shape[2]
    scale = 1.0 / (seqs * lax.axis_size("yh") * lax.axis_size("core"))
    me = (lax.axis_index("yh") * 2 + lax.axis_index("core")).astype(jnp.int32).reshape(1)
    source_x = ring_sources(lax.axis_index("x"))
    source_z = ring_sources(lax.axis_index("row"))

    mine = jnp.transpose(pair_cotangent, (1, 0, 2))
    across = depth_exchange(mine, 1, 0)
    beside = depth_exchange(mine, 0, 1)
    ap = left_factor.reshape(seqs, chans * rows)
    bt = jnp.transpose(right_factor, (2, 1, 0)).reshape(cols * chans, seqs)
    across, ap, bt = lax.optimization_barrier((across, ap, bt))
    both = depth_exchange(across, 0, 1)
    pieces = (mine, beside, across, both)

    delta, keep_a, send_a, keep_b, send_b = left_call(me, source_x, pieces, out_weight, bt, chans)
    came = (swap(send_a, "x", 0), swap(send_b, "x", 1))
    weight_part = weight_call(me, pieces, bt, ap, chans)
    came, weight_part = lax.optimization_barrier((came, weight_part))

    cut = seqs // 4
    keep = (join(keep_a[:, :cut], came[0][:, :cut]), join(keep_b[:, :cut], came[1][:, :cut]))
    send = (join(keep_a[:, cut:], came[0][:, cut:]), join(keep_b[:, cut:], came[1][:, cut:]))
    came = (swap(send[0], "x", 1), swap(send[1], "x", 0))
    send, ap = lax.optimization_barrier((send, ap))
    right_parts = right_call(source_z, ap, delta)
    came, right_parts = lax.optimization_barrier((came, right_parts))
    keep_a, send_a, keep_b, send_b = right_parts
    right_came = (swap(send_a, "row", 0), swap(send_b, "row", 1))

    yl = lax.axis_index("yl")
    both_keep = [k.reshape(CHUNKS // 2, 2, cut // 2, -1) for k in keep]
    both_came = [c.reshape(CHUNKS // 2, 2, cut // 2, -1) for c in came]

    def take(at, dtype):
        parts = []
        for k, c in zip(both_keep, both_came):
            k = lax.dynamic_index_in_dim(k, at, 1, keepdims=False)
            c = lax.dynamic_index_in_dim(c, at, 1, keepdims=False)
            parts.append(join(k, c, dtype))
        return jnp.concatenate(parts, axis=0)

    left_came = swap(take(1 - yl, BF16), "yl")
    left_keep = take(yl, F32)

    send_end = (join(keep_a[cut:], right_came[0][cut:]), join(keep_b[cut:], right_came[1][cut:]))
    keep_end = (join(keep_a[:cut], right_came[0][:cut]), join(keep_b[:cut], right_came[1][:cut]))
    weight = summed(weight_part, EVERY) * scale
    right_last = (swap(send_end[0], "row", 1), swap(send_end[1], "row", 0))

    left_grad = left_end_call(left_keep, left_came, chans, scale)
    right_grad = right_end_call(keep_end[0], right_last[0], keep_end[1], right_last[1], chans, scale)
    return left_grad, jnp.transpose(right_grad, (2, 0, 1)), weight


def solution(mesh):
    finer = Mesh(mesh.devices.reshape(2, 2, mesh.shape["row"], 4, 2), EVERY)
    in_specs = (P(DEPTH, None, "row"), P(DEPTH, None, COL), P(), P(("row",) + DEPTH, COL, None))
    out_specs = (P(DEPTH + COL, None, "row"), P(DEPTH + ("row",), None, COL), P(EVERY, None))
    return jax.shard_map(body, mesh=finer, in_specs=in_specs, out_specs=out_specs, check_vma=False)
```

time: 183 us -> 122 us (0.67)
  waiting for transfers between devices: 48.4 us -> 15.1 us
  blocking collectives: 27.8 us -> 0 us
  starting transfers between devices: 18.2 us -> 27.9 us
  local copies, waits for them, and re-layouts: 20.2 us -> 13 us
  Pallas kernels: 62.7 us -> 59.4 us
  other arithmetic: 3.94 us -> 5.85 us
    all_to_all x2 -> x1, waiting for transfers between devices: 48.4 us -> 0.01 us  [summed(): blocks = lax.all_to_all(blocks, axes, 0, 0, tiled=True)]
    all_to_all x1 -> x0, blocking collectives: 27.8 us -> none  [summed(): blocks = lax.all_to_all(blocks, axes, 0, 0, tiled=True)]
    ppermute x0 -> x9, starting transfers between devices: none -> 14.5 us  [swap(): return lax.ppermute(array, axis, pairs)]
    ppermute x0 -> x9, waiting for transfers between devices: none -> 11.3 us  [swap(): return lax.ppermute(array, axis, pairs)]
    pallas_call x2 -> x3, Pallas kernels: 27.4 us -> 19.9 us  [the longest x1 13.7 us: right_call(): pl.pallas_call(right_kernel, grid=(k // tile,), in_specs=[pl.BlockSpec(me...]
    pallas_call x1, Pallas kernels: 11.9 us -> 17.7 us  [weight_call(): pl.pallas_call(functools.partial(weight_kernel, chans), grid=(cols // her...]
    all_to_all x2 -> x1, starting transfers between devices: 14.3 us -> 10 us  [summed(): blocks = lax.all_to_all(blocks, axes, 0, 0, tiled=True)]
    ppermute x3, waiting for transfers between devices: 0.01 us -> 3.78 us  [depth_exchange(): return lax.ppermute(array, DEPTH, pairs)]
  transfers between devices with their start and end apart: 5 -> 13, of which waited for: 1 -> 6; matrix products, arithmetic and copies ran while one was open for 10% -> 12% of each run, Pallas kernels for 28% -> 28%
where the time goes in v2:
time: 122 us
  Pallas kernels  59.4 us (49%)
  starting transfers between devices  27.9 us (23%)
  waiting for transfers between devices  15.1 us (12%)
  local copies, waits for them, and re-layouts  13 us (11%)
  other arithmetic  5.85 us (5%)
    pallas_call x1, Pallas kernels, left_call(): pl.pallas_call(functools.partial(left_kernel, chans), grid=(steps,), in_s...  21.8 us
    pallas_call x1, Pallas kernels, weight_call(): pl.pallas_call(functools.partial(weight_kernel, chans), grid=(cols // her...  17.7 us
    ppermute x9, starting transfers between devices, swap(): return lax.ppermute(array, axis, pairs)  14.5 us
    pallas_call x1, Pallas kernels, right_call(): pl.pallas_call(right_kernel, grid=(k // tile,), in_specs=[pl.BlockSpec(me...  13.7 us
    ppermute x9, waiting for transfers between devices, swap(): return lax.ppermute(array, axis, pairs)  11.3 us
    all_to_all x1, starting transfers between devices, summed(): blocks = lax.all_to_all(blocks, axes, 0, 0, tiled=True)  10 us
    unnamed x26, local copies, waits for them, and re-layouts  8.94 us
    transpose x1, local copies, waits for them, and re-layouts, body(): bt = jnp.transpose(right_factor, (2, 1, 0)).reshape(cols * chans, seqs)  4.08 us
  transfers between devices with their start and end apart: 13, of which 6 were waited for; matrix products, arithmetic and copies ran while one was open for 12% of the time, Pallas kernels for 28%

profile of v2, /device:TPU:0, one launch (start us, length us, event | category | flops | bytes accessed | tf_op | source)
XLA Modules:
  0.0 122.0 jit_solution(9016557988551142750)
XLA Ops:
  0.6 1.5 %copy.31 = bf16[32,64,128]{2,0,1:T(8,128)(2,1)S(1)} copy(bf16[32,64,128]{2,1,0:T(8,128)(2,1)} %param.7) | data formatting | bytes 1048576 | tf_op args[3]
  2.2 3.4 %collective-permute-start.1 = (bf16[64,32,128]{2,1,0:T(8,128)(2,1)S(1)}, bf16[64,32,128]{2,1,0:T(8,128)(2,1)S(1)}, u32[]{:S(2)}, u32[]{:S(2)}) collective-permute-start(bf16[64,32,128]{2,1,0:T(8,128)(2,1)S(1)} %bitcast.57), channel_id=1, source_target_pairs={{0,64},{32,96},{64,0},{96,32},{1,65},{33,97},{65,1},{97,33},{2,66}... | collective-permute-start | bytes 1572872 | tf_op jit(solution)/shard_map/ppermute | solution.py:284
  5.5 4.1 %copy.10 = bf16[64,32,448]{2,1,0:T(8,128)(2,1)} copy(bf16[64,32,448]{2,0,1:T(8,128)(2,1)} %bitcast.51) | data formatting | bytes 3670016 | tf_op jit(solution)/shard_map/transpose | solution.py:336
  9.6 5.1 %copy.30 = bf16[56,8,32,128]{3,1,2,0:T(8,128)(2,1)} copy(bf16[56,8,32,128]{3,2,1,0:T(8,128)(2,1)S(1)} %bitcast.48) | data formatting | bytes 7340032
  14.7 2.7 %collective-permute-done.1.g2 = bf16[64,32,128]{2,1,0:T(8,128)(2,1)S(1)} collective-permute-done((bf16[64,32,128]{2,1,0:T(8,128)(2,1)S(1)}, bf16[64,32,128]{2,1,0:T(8,128)(2,1)S(1)}, u32[]{:S(2)}, u32[]{:S(2)}) %collective-permute-start.1) | collective-permute-done | bytes 524320 | tf_op jit(solution)/shard_map/ppermute | solution.py:284
  18.3 1.1 collective-permute-done.2.g3
  20.2 21.8 %left.1 = (bf16[2048,4096]{1,0:T(8,128)(2,1)}, bf16[4,224,512]{2,1,0:T(8,128)(2,1)}, bf16[4,224,512]{2,1,0:T(8,128)(2,1)}, bf16[4,224,512]{2,1,0:T(8,128)(2,1)}, bf16[4,224,512]{2,1,0:T(8,128)(2,1)}) custom-call(s32[1]{0:T(128)} %bitcast.me_ref, s32[4]{0:T(128)} %get-tuple-element.59.from_ref, bf16[64,32,128]{2,1,0:T(8,128)(2,1)} %bitcast.59, ...), custom_call_target="tpu_custom_call" | custom-call | flops 11811160064 | bytes 22282240 | tf_op jit(solution)/shard_map/left/pallas_call | solution.py:101
  42.0 1.6 %collective-permute-start.3 = (bf16[4,224,512]{2,1,0:T(8,128)(2,1)}, bf16[4,224,512]{2,1,0:T(8,128)(2,1)S(1)}, u32[]{:S(2)}, u32[]{:S(2)}) collective-permute-start(bf16[4,224,512]{2,1,0:T(8,128)(2,1)} %get-tuple-element.28), channel_id=1, source_target_pairs={{0,2},{2,0},{4,6},{6,4},{1,3},{3,1},{5,7},{7,5},{8,10},{10,8},{12,... | collective-permute-start | bytes 2752520 | tf_op jit(solution)/shard_map/ppermute | solution.py:308
  43.6 2.1 %collective-permute-start.4 = (bf16[4,224,512]{2,1,0:T(8,128)(2,1)}, bf16[4,224,512]{2,1,0:T(8,128)(2,1)S(1)}, u32[]{:S(2)}, u32[]{:S(2)}) collective-permute-start(bf16[4,224,512]{2,1,0:T(8,128)(2,1)} %get-tuple-element.29), channel_id=1, source_target_pairs={{0,6},{2,4},{4,2},{6,0},{1,7},{3,5},{5,3},{7,1},{8,14},{10,12},{12... | collective-permute-start | bytes 2752520 | tf_op jit(solution)/shard_map/ppermute | solution.py:308
  45.7 17.7 %weight.1 = bf16[1024,128]{1,0:T(8,128)(2,1)} custom-call(s32[1]{0:T(128)} %bitcast.me_ref, bf16[64,32,128]{2,1,0:T(8,128)(2,1)} %bitcast.60, bf16[64,32,128]{2,1,0:T(8,128)(2,1)} %copy-done.10, bf16[64,32,128]{2,1,0:T(8,128)(2,1)} %copy-done.9, bf16[64,32,128]{2,1,0:T(8,128)(2,1)} %copy-done.11, bf16[2048,448]{1,0:T(8,128)(2,1)} %bitcast.53, ...), custom_call_target="tpu_custom_call" | custom-call | flops 11811160064 | bytes 5505024 | tf_op jit(solution)/shard_map/weight/pallas_call | solution.py:257
  63.3 1.3 %collective-permute-done.3 = bf16[4,224,512]{2,1,0:T(8,128)(2,1)S(1)} collective-permute-done((bf16[4,224,512]{2,1,0:T(8,128)(2,1)}, bf16[4,224,512]{2,1,0:T(8,128)(2,1)S(1)}, u32[]{:S(2)}, u32[]{:S(2)}) %collective-permute-start.3) | collective-permute-done | bytes 917536 | tf_op jit(solution)/shard_map/ppermute | solution.py:308
  64.6 2.5 %collective-permute-done.4 = bf16[4,224,512]{2,1,0:T(8,128)(2,1)S(1)} collective-permute-done((bf16[4,224,512]{2,1,0:T(8,128)(2,1)}, bf16[4,224,512]{2,1,0:T(8,128)(2,1)S(1)}, u32[]{:S(2)}, u32[]{:S(2)}) %collective-permute-start.4) | collective-permute-done | bytes 917536 | tf_op jit(solution)/shard_map/ppermute | solution.py:308
  67.5 1.0 add_convert_fusion.3
  68.5 2.1 %collective-permute-start.5 = (bf16[4,112,512]{2,1,0:T(8,128)(2,1)}, bf16[4,112,512]{2,1,0:T(8,128)(2,1)S(1)}, u32[]{:S(2)}, u32[]{:S(2)}) collective-permute-start(bf16[4,112,512]{2,1,0:T(8,128)(2,1)} %get-tuple-element.48), channel_id=1, source_target_pairs={{0,6},{2,4},{4,2},{6,0},{1,7},{3,5},{5,3},{7,1},{8,14},{10,12},{12... | collective-permute-start | bytes 1376264 | tf_op jit(solution)/shard_map/ppermute | solution.py:308
  70.6 10.0 %all-to-all-start = ((bf16[128,8,128]{2,1,0:T(8,128)(2,1)}), bf16[128,8,128]{2,1,0:T(8,128)(2,1)S(1)}, u32[]{:S(2)}, u32[]{:S(2)}) async-start(bf16[128,8,128]{2,1,0:T(8,128)(2,1)} %bitcast.21), calls=%async_computation | async-start | bytes 524288 | tf_op jit(solution)/shard_map/all_to_all | solution.py:320
  80.6 13.7 %right.1 = (bf16[224,1024]{1,0:T(8,128)(2,1)}, bf16[224,1024]{1,0:T(8,128)(2,1)}, bf16[224,1024]{1,0:T(8,128)(2,1)}, bf16[224,1024]{1,0:T(8,128)(2,1)}) custom-call(s32[4]{0:T(128)} %get-tuple-element.60.from_ref, bf16[448,4096]{1,0:T(8,128)(2,1)} %bitcast.50, bf16[2048,4096]{1,0:T(8,128)(2,1)} %get-tuple-element.35.delta_ref), custom_call_target="tpu_custom_call" | custom-call | flops 7516192768 | bytes 22282240 | tf_op jit(solution)/shard_map/right/pallas_call | solution.py:160
  94.3 1.2 collective-permute-start.8
  95.6 2.4 %collective-permute-start.10 = (bf16[224,1024]{1,0:T(8,128)(2,1)}, bf16[224,1024]{1,0:T(8,128)(2,1)S(1)}, u32[]{:S(2)}, u32[]{:S(2)}) collective-permute-start(bf16[224,1024]{1,0:T(8,128)(2,1)} %get-tuple-element.45), channel_id=1, source_target_pairs={{0,24},{8,16},{16,8},{24,0},{1,25},{9,17},{17,9},{25,1},{2,26},{10... | collective-permute-start | bytes 1376264 | tf_op jit(solution)/shard_map/ppermute | solution.py:308
  98.3 1.6 %collective-permute-start.7 = (bf16[8,56,512]{2,1,0:T(8,128)(2,1)S(1)}, bf16[8,56,512]{2,1,0:T(8,128)(2,1)S(1)}, u32[]{:S(2)}, u32[]{:S(2)}) collective-permute-start(bf16[8,56,512]{2,1,0:T(8,128)(2,1)S(1)} %pad_maximum_fusion.1), channel_id=1, source_target_pairs={{0,1},{1,0},{2,3},{3,2},{4,5},{5,4},{6,7},{7,6},{8,9},{9,8},{10,11... | collective-permute-start | bytes 1376264 | tf_op jit(solution)/shard_map/ppermute | solution.py:308
  99.9 6.6 %collective-permute-done.8 = bf16[224,1024]{1,0:T(8,128)(2,1)S(1)} collective-permute-done((bf16[224,1024]{1,0:T(8,128)(2,1)}, bf16[224,1024]{1,0:T(8,128)(2,1)S(1)}, u32[]{:S(2)}, u32[]{:S(2)}) %collective-permute-start.8) | collective-permute-done | bytes 458784 | tf_op jit(solution)/shard_map/ppermute | solution.py:308
  107.4 3.5 %collective-permute-start.9 = (bf16[112,1024]{1,0:T(8,128)(2,1)S(1)}, bf16[112,1024]{1,0:T(8,128)(2,1)S(1)}, u32[]{:S(2)}, u32[]{:S(2)}) collective-permute-start(bf16[112,1024]{1,0:T(8,128)(2,1)S(1)} %get-tuple-element.53), channel_id=1, source_target_pairs={{0,24},{8,16},{16,8},{24,0},{1,25},{9,17},{17,9},{25,1},{2,26},{10... | collective-permute-start | bytes 688136 | tf_op jit(solution)/shard_map/ppermute | solution.py:308
  114.1 3.2 %left_end.1 = f32[56,32,128]{2,1,0:T(8,128)} custom-call(f32[8,56,512]{2,1,0:T(8,128)} %pad_maximum_fusion.keep_ref, bf16[8,56,512]{2,1,0:T(8,128)(2,1)} %copy-done.6), custom_call_target="tpu_custom_call" | custom-call | flops 458752 | bytes 2293760 | tf_op jit(solution)/shard_map/left_end/pallas_call | solution.py:189
  117.3 1.0 collective-permute-done.11.came_b
  119.0 3.1 %right_end.1 = f32[32,64,112]{2,1,0:T(8,128)} custom-call(bf16[112,1024]{1,0:T(8,128)(2,1)} %get-tuple-element.54.keep_a, bf16[112,1024]{1,0:T(8,128)(2,1)} %copy-done.7, bf16[112,1024]{1,0:T(8,128)(2,1)} %get-tuple-element.52.keep_b, bf16[112,1024]{1,0:T(8,128)(2,1)} %copy-done.8), custom_call_target="tpu_custom_call" | custom-call | flops 458752 | bytes 1835008 | tf_op jit(solution)/shard_map/right_end/pallas_call | solution.py:212
  (45 shorter events, 7.2 us)
Async XLA Ops:
  0.6 9.0 %copy-start = (bf16[448,32,128]{2,1,0:T(8,128)(2,1)S(1)}, bf16[448,32,128]{2,1,0:T(8,128)(2,1)}, u32[]{:S(2)}) copy-start(bf16[448,32,128]{2,1,0:T(8,128)(2,1)} %param.4) | copy-start | bytes 11010052
  2.2 12.6 %copy-start.3 = (bf16[32,64,128]{2,0,1:T(8,128)(2,1)}, bf16[32,64,128]{2,0,1:T(8,128)(2,1)S(1)}, u32[]{:S(2)}) copy-start(bf16[32,64,128]{2,0,1:T(8,128)(2,1)S(1)} %copy.31) | copy-start | bytes 1572868
  2.2 15.3 %collective-permute-start.1 = (bf16[64,32,128]{2,1,0:T(8,128)(2,1)S(1)}, bf16[64,32,128]{2,1,0:T(8,128)(2,1)S(1)}, u32[]{:S(2)}, u32[]{:S(2)}) collective-permute-start(bf16[64,32,128]{2,1,0:T(8,128)(2,1)S(1)} %bitcast.57), channel_id=1, source_target_pairs={{0,64},{32,96},{64,0},{96,32},{1,65},{33,97},{65,1},{97,33},{2,66}... | collective-permute-start | bytes 1572872 | tf_op jit(solution)/shard_map/ppermute | solution.py:284
  5.5 12.8 %collective-permute-start = (bf16[64,32,128]{2,1,0:T(8,128)(2,1)S(1)}, bf16[64,32,128]{2,1,0:T(8,128)(2,1)S(1)}, u32[]{:S(2)}, u32[]{:S(2)}) collective-permute-start(bf16[64,32,128]{2,1,0:T(8,128)(2,1)S(1)} %bitcast.58), channel_id=1, source_target_pairs={{0,32},{32,0},{64,96},{96,64},{1,33},{33,1},{65,97},{97,65},{2,34}... | collective-permute-start | bytes 1572872 | tf_op jit(solution)/shard_map/ppermute | solution.py:284
  17.5 1.9 %copy-start.9 = (bf16[64,32,128]{2,1,0:T(8,128)(2,1)}, bf16[64,32,128]{2,1,0:T(8,128)(2,1)S(1)}, u32[]{:S(2)}) copy-start(bf16[64,32,128]{2,1,0:T(8,128)(2,1)S(1)} %collective-permute-done.1.g2) | copy-start | bytes 1572868
  17.5 1.9 %collective-permute-start.2 = (bf16[64,32,128]{2,1,0:T(8,128)(2,1)S(1)}, bf16[64,32,128]{2,1,0:T(8,128)(2,1)S(1)}, u32[]{:S(2)}, u32[]{:S(2)}) collective-permute-start(bf16[64,32,128]{2,1,0:T(8,128)(2,1)S(1)} %collective-permute-done.1.g2), channel_id=1, source_target_pairs={{0,32},{32,0},{64,96},{96,64},{1,33},{33,1},{65,97},{97,65},{2,34}... | collective-permute-start | bytes 1572872 | tf_op jit(solution)/shard_map/ppermute | solution.py:284
  18.3 1.1 copy-start.10
  19.4 0.8 copy-start.11
  42.0 22.6 %collective-permute-start.3 = (bf16[4,224,512]{2,1,0:T(8,128)(2,1)}, bf16[4,224,512]{2,1,0:T(8,128)(2,1)S(1)}, u32[]{:S(2)}, u32[]{:S(2)}) collective-permute-start(bf16[4,224,512]{2,1,0:T(8,128)(2,1)} %get-tuple-element.28), channel_id=1, source_target_pairs={{0,2},{2,0},{4,6},{6,4},{1,3},{3,1},{5,7},{7,5},{8,10},{10,8},{12,... | collective-permute-start | bytes 2752520 | tf_op jit(solution)/shard_map/ppermute | solution.py:308
  43.6 23.5 %copy-start.2 = (bf16[4,224,512]{2,1,0:T(8,128)(2,1)S(1)}, bf16[4,224,512]{2,1,0:T(8,128)(2,1)}, u32[]{:S(2)}) copy-start(bf16[4,224,512]{2,1,0:T(8,128)(2,1)} %get-tuple-element.32) | copy-start | bytes 2752516
  43.6 23.9 %copy-start.1 = (bf16[4,224,512]{2,1,0:T(8,128)(2,1)S(1)}, bf16[4,224,512]{2,1,0:T(8,128)(2,1)}, u32[]{:S(2)}) copy-start(bf16[4,224,512]{2,1,0:T(8,128)(2,1)} %get-tuple-element.27) | copy-start | bytes 2752516
  43.6 23.5 %collective-permute-start.4 = (bf16[4,224,512]{2,1,0:T(8,128)(2,1)}, bf16[4,224,512]{2,1,0:T(8,128)(2,1)S(1)}, u32[]{:S(2)}, u32[]{:S(2)}) collective-permute-start(bf16[4,224,512]{2,1,0:T(8,128)(2,1)} %get-tuple-element.29), channel_id=1, source_target_pairs={{0,6},{2,4},{4,2},{6,0},{1,7},{3,5},{5,3},{7,1},{8,14},{10,12},{12... | collective-permute-start | bytes 2752520 | tf_op jit(solution)/shard_map/ppermute | solution.py:308
  67.3 26.9 %collective-permute-start.6 = (bf16[4,112,512]{2,1,0:T(8,128)(2,1)S(1)}, bf16[4,112,512]{2,1,0:T(8,128)(2,1)S(1)}, u32[]{:S(2)}, u32[]{:S(2)}) collective-permute-start(bf16[4,112,512]{2,1,0:T(8,128)(2,1)S(1)} %get-tuple-element.50), channel_id=1, source_target_pairs={{0,2},{2,0},{4,6},{6,4},{1,3},{3,1},{5,7},{7,5},{8,10},{10,8},{12,... | collective-permute-start | bytes 1376264 | tf_op jit(solution)/shard_map/ppermute | solution.py:308
  68.5 25.8 %collective-permute-start.5 = (bf16[4,112,512]{2,1,0:T(8,128)(2,1)}, bf16[4,112,512]{2,1,0:T(8,128)(2,1)S(1)}, u32[]{:S(2)}, u32[]{:S(2)}) collective-permute-start(bf16[4,112,512]{2,1,0:T(8,128)(2,1)} %get-tuple-element.48), channel_id=1, source_target_pairs={{0,6},{2,4},{4,2},{6,0},{1,7},{3,5},{5,3},{7,1},{8,14},{10,12},{12... | collective-permute-start | bytes 1376264 | tf_op jit(solution)/shard_map/ppermute | solution.py:308
  70.6 24.9 %all-to-all-start = ((bf16[128,8,128]{2,1,0:T(8,128)(2,1)}), bf16[128,8,128]{2,1,0:T(8,128)(2,1)S(1)}, u32[]{:S(2)}, u32[]{:S(2)}) async-start(bf16[128,8,128]{2,1,0:T(8,128)(2,1)} %bitcast.21), calls=%async_computation | async-start | bytes 524288 | tf_op jit(solution)/shard_map/all_to_all | solution.py:320
  94.3 12.2 %copy-start.5 = (bf16[224,1024]{1,0:T(8,128)(2,1)S(1)}, bf16[224,1024]{1,0:T(8,128)(2,1)}, u32[]{:S(2)}) copy-start(bf16[224,1024]{1,0:T(8,128)(2,1)} %get-tuple-element.42) | copy-start | bytes 1376260
  94.3 16.6 %copy-start.4 = (bf16[224,1024]{1,0:T(8,128)(2,1)S(1)}, bf16[224,1024]{1,0:T(8,128)(2,1)}, u32[]{:S(2)}) copy-start(bf16[224,1024]{1,0:T(8,128)(2,1)} %get-tuple-element.44) | copy-start | bytes 1376260
  94.3 12.2 %collective-permute-start.8 = (bf16[224,1024]{1,0:T(8,128)(2,1)}, bf16[224,1024]{1,0:T(8,128)(2,1)S(1)}, u32[]{:S(2)}, u32[]{:S(2)}) collective-permute-start(bf16[224,1024]{1,0:T(8,128)(2,1)} %get-tuple-element.43), channel_id=1, source_target_pairs={{0,8},{8,0},{16,24},{24,16},{1,9},{9,1},{17,25},{25,17},{2,10},{10... | collective-permute-start | bytes 1376264 | tf_op jit(solution)/shard_map/ppermute | solution.py:308
  95.6 15.3 %collective-permute-start.10 = (bf16[224,1024]{1,0:T(8,128)(2,1)}, bf16[224,1024]{1,0:T(8,128)(2,1)S(1)}, u32[]{:S(2)}, u32[]{:S(2)}) collective-permute-start(bf16[224,1024]{1,0:T(8,128)(2,1)} %get-tuple-element.45), channel_id=1, source_target_pairs={{0,24},{8,16},{16,8},{24,0},{1,25},{9,17},{17,9},{25,1},{2,26},{10... | collective-permute-start | bytes 1376264 | tf_op jit(solution)/shard_map/ppermute | solution.py:308
  98.3 15.0 %collective-permute-start.7 = (bf16[8,56,512]{2,1,0:T(8,128)(2,1)S(1)}, bf16[8,56,512]{2,1,0:T(8,128)(2,1)S(1)}, u32[]{:S(2)}, u32[]{:S(2)}) collective-permute-start(bf16[8,56,512]{2,1,0:T(8,128)(2,1)S(1)} %pad_maximum_fusion.1), channel_id=1, source_target_pairs={{0,1},{1,0},{2,3},{3,2},{4,5},{5,4},{6,7},{7,6},{8,9},{9,8},{10,11... | collective-permute-start | bytes 1376264 | tf_op jit(solution)/shard_map/ppermute | solution.py:308
  107.4 9.9 %collective-permute-start.9 = (bf16[112,1024]{1,0:T(8,128)(2,1)S(1)}, bf16[112,1024]{1,0:T(8,128)(2,1)S(1)}, u32[]{:S(2)}, u32[]{:S(2)}) collective-permute-start(bf16[112,1024]{1,0:T(8,128)(2,1)S(1)} %get-tuple-element.53), channel_id=1, source_target_pairs={{0,24},{8,16},{16,8},{24,0},{1,25},{9,17},{17,9},{25,1},{2,26},{10... | collective-permute-start | bytes 688136 | tf_op jit(solution)/shard_map/ppermute | solution.py:308
  111.7 6.5 %collective-permute-start.11 = (bf16[112,1024]{1,0:T(8,128)(2,1)S(1)}, bf16[112,1024]{1,0:T(8,128)(2,1)S(1)}, u32[]{:S(2)}, u32[]{:S(2)}) collective-permute-start(bf16[112,1024]{1,0:T(8,128)(2,1)S(1)} %get-tuple-element.51), channel_id=1, source_target_pairs={{0,8},{8,0},{16,24},{24,16},{1,9},{9,1},{17,25},{25,17},{2,10},{10... | collective-permute-start | bytes 688136 | tf_op jit(solution)/shard_map/ppermute | solution.py:308
  113.3 0.8 copy-start.6
  117.3 1.0 copy-start.7
  (1 other events, 0.7 us)

commit v3 on v2

v3 whole, which is shorter than its diff:
```python
import functools

import jax
import jax.numpy as jnp
from jax import lax
from jax.experimental import pallas as pl
from jax.experimental.pallas import tpu as pltpu
from jax.sharding import Mesh
from jax.sharding import PartitionSpec as P

BF16 = jnp.bfloat16
F32 = jnp.float32
COL = ("x", "yl")
DEPTH = ("yh", "core")
EVERY = ("yh", "core", "row", "x", "yl")
NT = (((1,), (1,)), ((), ()))
CHUNKS = 8
VMEM_LIMIT = 56 * 1024 * 1024


def params():
    return pltpu.CompilerParams(vmem_limit_bytes=VMEM_LIMIT)


def cost(flops, moved):
    return pl.CostEstimate(flops=flops, bytes_accessed=moved, transcendentals=0)


def place_pieces(me_ref, pieces, pairs_ref):
    rows = pieces[0].shape[1]
    for step, piece in enumerate(pieces):
        at = pl.multiple_of(jnp.bitwise_xor(me_ref[0], step) * rows, rows)
        pairs_ref[:, pl.ds(at, rows), :] = piece[...]


def pair_kernel(chans, me_ref, x_ref, z_ref, g0, g1, g2, g3, w_ref, bp_ref, a_ref, *rest):
    keep_a, send_a, keep_b, send_b = rest[:4]
    right_refs = rest[4:8]
    pairs_ref, b_ref, delta_ref = rest[8:]
    width = pairs_ref.shape[1]
    rows = bp_ref.shape[0] // 4
    place_pieces(me_ref, (g0, g1, g2, g3), pairs_ref)
    for q in range(4):
        start = pl.multiple_of(x_ref[q] * rows, 16)
        b_ref[q * rows : (q + 1) * rows, :] = bp_ref[pl.ds(start, rows), :]

    here = 8
    many = 16
    for first in range(0, chans, here):
        w = w_ref[first * chans : (first + here) * chans, :]

        def step(t, carry, w=w, first=first):
            g = pairs_ref[pl.ds(many * t, many)].reshape(many * width, -1)
            d = lax.dot_general(w, g, NT, preferred_element_type=F32).astype(BF16)
            for u in range(many):
                at = pl.ds(pl.multiple_of((many * t + u) * chans, chans), chans)
                for c in range(here):
                    delta_ref[at, (first + c) * width : (first + c + 1) * width] = d[
                        c * chans : (c + 1) * chans, u * width : (u + 1) * width
                    ]
            return carry

        lax.fori_loop(0, pairs_ref.shape[0] // many, step, 0, unroll=2)

    chunks, _, tile = keep_a.shape
    per = here * width // tile
    for at in range(0, 2 * chunks, per):
        total = jnp.dot(b_ref[...], delta_ref[:, at * tile : (at + per) * tile], preferred_element_type=F32)
        total = total.astype(BF16)
        for q in range(per):
            cut = slice(q * tile, (q + 1) * tile)
            if at < chunks:
                keep_a[at + q] = total[: 2 * rows, cut]
                send_a[at + q] = total[2 * rows :, cut]
            else:
                for half in range(2):
                    low = 2 * half * rows
                    to = slice(half * rows, (half + 1) * rows)
                    keep_b[at + q - chunks, to] = total[low : low + rows, cut]
                    send_b[at + q - chunks, to] = total[low + rows : low + 2 * rows, cut]

    strip = 512
    for at in range(0, delta_ref.shape[0], strip):
        a = jnp.concatenate(
            [a_ref[pl.ds(pl.multiple_of(z_ref[q] * rows, 16), rows), :] for q in range(4)], axis=0
        )
        part = lax.dot_general(a, delta_ref[at : at + strip, :], NT, preferred_element_type=F32)
        for q in range(4):
            right_refs[q][:, at : at + strip] = part[q * rows : (q + 1) * rows].astype(BF16)


def pair_call(me, source_x, source_z, pieces, w, bp, ap, chans):
    cols, rows, pair = pieces[0].shape
    width = 4 * rows
    seqs, k = bp.shape
    n = chans * width
    smem = pl.BlockSpec(memory_space=pltpu.SMEM)
    vmem = pl.BlockSpec(memory_space=pltpu.VMEM)
    left = (CHUNKS // 2, seqs // 2, n // CHUNKS)
    right = (seqs // 4, k)
    return pl.pallas_call(
        functools.partial(pair_kernel, chans),
        in_specs=[smem] * 3 + [vmem] * 7,
        out_specs=[vmem] * 8,
        out_shape=[jax.ShapeDtypeStruct(left, BF16)] * 4 + [jax.ShapeDtypeStruct(right, BF16)] * 4,
        scratch_shapes=[
            pltpu.VMEM((cols, width, pair), BF16),
            pltpu.VMEM((seqs, k), BF16),
            pltpu.VMEM((k, n), BF16),
        ],
        compiler_params=params(),
        cost_estimate=cost(2 * k * n * (pair * 2 + 2 * seqs), 2 * (2 * seqs * n + seqs * k)),
        name="pair",
    )(me, source_x, source_z, *pieces, w, bp, ap)


def left_end_kernel(scale, keep_a, came_a, keep_b, came_b, out_ref):
    chunks, _, tile = keep_a.shape
    width = out_ref.shape[2]
    per = tile // width
    for at, (keep, came) in enumerate(((keep_a, came_a), (keep_b, came_b))):
        for q in range(chunks):
            total = (keep[q].astype(F32) + came[q].astype(F32)) * scale
            for c in range(per):
                out_ref[:, (at * chunks + q) * per + c, :] = total[:, c * width : (c + 1) * width]


def left_end_call(keep, came, chans, scale):
    chunks, seqs, tile = keep[0].shape
    size = keep[0].size
    return pl.pallas_call(
        functools.partial(left_end_kernel, scale),
        out_shape=jax.ShapeDtypeStruct((seqs, chans, 2 * chunks * tile // chans), F32),
        compiler_params=params(),
        cost_estimate=cost(4 * size, 16 * size),
        name="left_end",
    )(keep[0], came[0], keep[1], came[1])


def right_end_kernel(scale, p0, p1, p2, p3, out_ref, turned_ref):
    chans, cols, _ = out_ref.shape
    for k in range(0, chans * cols, 128):
        parts = [p[:, k : k + 128].astype(F32) for p in (p0, p1, p2, p3)]
        total = ((parts[0] + parts[1]) + (parts[2] + parts[3])) * scale
        turned_ref[k : k + 128, :] = jnp.pad(total, ((0, 128 - total.shape[0]), (0, 0))).T
    for e in range(chans):
        out_ref[e] = turned_ref[pl.ds(e, cols, stride=chans), :][:, : out_ref.shape[2]]


def right_end_call(parts, chans, scale):
    seqs, n = parts[0].shape
    return pl.pallas_call(
        functools.partial(right_end_kernel, scale),
        out_shape=jax.ShapeDtypeStruct((chans, n // chans, seqs), F32),
        scratch_shapes=[pltpu.VMEM((n, 128), F32)],
        compiler_params=params(),
        cost_estimate=cost(4 * parts[0].size, 12 * parts[0].size),
        name="right_end",
    )(*parts)


def weight_kernel(chans, me_ref, g0, g1, g2, g3, bt_ref, a_ref, out_ref, pairs_ref, acc_ref):
    step = pl.program_id(0)
    width = pairs_ref.shape[1]

    @pl.when(step == 0)
    def _():
        place_pieces(me_ref, (g0, g1, g2, g3), pairs_ref)
        acc_ref[...] = jnp.zeros_like(acc_ref)

    here = bt_ref.shape[0] // chans
    g = pairs_ref[pl.ds(step * here, here)].reshape(here * width, -1)
    group = 8
    for q in range(chans // group):
        a = a_ref[:, q * group * width : (q + 1) * group * width]
        outer = jnp.dot(bt_ref[...], a, preferred_element_type=F32).astype(BF16)
        parts = []
        for u in range(here):
            rows = outer[u * chans : (u + 1) * chans]
            parts.append(jnp.concatenate([rows[:, c * width : (c + 1) * width] for c in range(group)], axis=0))
        acc_ref[q * group * chans : (q + 1) * group * chans, :] += jnp.dot(
            jnp.concatenate(parts, axis=1), g, preferred_element_type=F32
        )

    @pl.when(step == pl.num_programs(0) - 1)
    def _():
        out_ref[...] = acc_ref[...].astype(BF16)


def weight_call(me, pieces, bt, ap, chans):
    cols, rows, pair = pieces[0].shape
    width = 4 * rows
    k, seqs = bt.shape
    n = ap.shape[1]
    here = 16
    whole = pl.BlockSpec((cols, rows, pair), lambda g: (0, 0, 0))
    return pl.pallas_call(
        functools.partial(weight_kernel, chans),
        grid=(cols // here,),
        in_specs=[
            pl.BlockSpec(memory_space=pltpu.SMEM),
            whole,
            whole,
            whole,
            whole,
            pl.BlockSpec((here * chans, seqs), lambda g: (g, 0)),
            pl.BlockSpec((seqs, n), lambda g: (0, 0)),
        ],
        out_specs=pl.BlockSpec((chans * chans, pair), lambda g: (0, 0)),
        out_shape=jax.ShapeDtypeStruct((chans * chans, pair), BF16),
        scratch_shapes=[pltpu.VMEM((cols, width, pair), BF16), pltpu.VMEM((chans * chans, pair), F32)],
        compiler_params=params(),
        cost_estimate=cost(2 * k * n * (seqs + 2 * pair), 2 * (k * seqs + n * seqs)),
        name="weight",
    )(me, *pieces, bt, ap)


def depth_exchange(array, other_chip, other_core):
    pairs = []
    for chip in range(2):
        for core in range(2):
            to = (chip ^ other_chip) * 2 + (core ^ other_core)
            pairs.append((chip * 2 + core, to))
    return lax.ppermute(array, DEPTH, pairs)


def ring_partner(at, bit):
    return at ^ 1 if bit == 0 else 3 - at


def ring_place(at, bits):
    for bit in (0, 1):
        if bits[bit]:
            at = ring_partner(at, bit)
    return at


def ring_sources(at):
    here = [ring_place(at, (first, second)) for first in (0, 1) for second in (0, 1)]
    return jnp.stack(here).astype(jnp.int32)


def swap(array, axis, bit=None):
    if bit is None:
        pairs = [(0, 1), (1, 0)]
    else:
        pairs = [(at, ring_partner(at, bit)) for at in range(4)]
    return lax.ppermute(array, axis, pairs)


def join(keep, came, dtype=BF16):
    return (keep.astype(F32) + came.astype(F32)).astype(dtype)


def body(left_factor, right_factor, out_weight, pair_cotangent):
    seqs, chans, rows = left_factor.shape
    cols = right_factor.shape[2]
    scale = 1.0 / (seqs * lax.axis_size("yh") * lax.axis_size("core"))
    me = (lax.axis_index("yh") * 2 + lax.axis_index("core")).astype(jnp.int32).reshape(1)
    source_x = ring_sources(lax.axis_index("x"))
    source_z = ring_sources(lax.axis_index("row"))

    mine = jnp.transpose(pair_cotangent, (1, 0, 2))
    across = depth_exchange(mine, 1, 0)
    beside = depth_exchange(mine, 0, 1)
    ap = left_factor.reshape(seqs, chans * rows)
    bt = jnp.transpose(right_factor, (2, 1, 0)).reshape(cols * chans, seqs)
    bt = lax.optimization_barrier(bt)
    across, ap, bt, bp = lax.optimization_barrier((across, ap, bt, bt.T))
    both = depth_exchange(across, 0, 1)
    pieces = (mine, beside, across, both)

    keep_a, send_a, keep_b, send_b, *right_parts = pair_call(
        me, source_x, source_z, pieces, out_weight, bp, ap, chans
    )
    came_a, came_b = swap(send_a, "x", 0), swap(send_b, "x", 1)
    right_came = [right_parts[0]]
    for q in (3, 1, 2):
        pairs = [(at, ring_place(at, divmod(q, 2))) for at in range(4)]
        right_came.append(lax.ppermute(right_parts[q], "row", pairs))
    weight_part = weight_call(me, pieces, bt, ap, chans)
    came_a, came_b, right_came, weight_part = lax.optimization_barrier((came_a, came_b, right_came, weight_part))

    yl = lax.axis_index("yl")
    cut = seqs // 8

    def by_place(array):
        return array.reshape(CHUNKS // 2, 2, 2, cut, -1)

    keep_a, came_a, keep_b, came_b = by_place(keep_a), by_place(came_a), by_place(keep_b), by_place(came_b)

    def take(array, axis, at):
        return lax.dynamic_index_in_dim(array, at, axis, keepdims=False)

    send_b = join(keep_b[:, 1], came_b[:, 1])
    send_a = join(take(keep_a, 2, 1 - yl), take(came_a, 2, 1 - yl))
    came_b2 = swap(send_b, "x", 0)
    came_a2 = swap(send_a, "yl")
    keep_a = join(take(keep_a, 2, yl), take(came_a, 2, yl), F32)
    keep_b = join(keep_b[:, 0], came_b[:, 0], F32)
    keep_a, keep_b, weight_part = lax.optimization_barrier((keep_a, keep_b, weight_part))
    blocks = lax.all_to_all(weight_part.reshape(128, -1, weight_part.shape[1]), EVERY, 0, 0, tiled=True)
    right_grad = right_end_call(right_came, chans, scale)

    came_a = swap(join(keep_a[:, 1], came_a2[:, 1]), "x", 1)
    came_b = swap(join(take(keep_b, 1, 1 - yl), take(came_b2, 1, 1 - yl)), "yl")
    keep_a = join(keep_a[:, 0], came_a2[:, 0], F32)
    keep_b = join(take(keep_b, 1, yl), take(came_b2, 1, yl), F32)
    left_grad = left_end_call((keep_a, keep_b), (came_a, came_b), chans, scale)
    blocks, left_grad, right_grad = lax.optimization_barrier((blocks, left_grad, right_grad))
    weight = jnp.sum(blocks.astype(F32), axis=0) * scale
    return left_grad, jnp.transpose(right_grad, (2, 0, 1)), weight


def solution(mesh):
    finer = Mesh(mesh.devices.reshape(2, 2, mesh.shape["row"], 4, 2), EVERY)
    in_specs = (P(DEPTH, None, "row"), P(DEPTH, None, COL), P(), P(("row",) + DEPTH, COL, None))
    out_specs = (P(DEPTH + COL, None, "row"), P(DEPTH + ("row",), None, COL), P(EVERY, None))
    return jax.shard_map(body, mesh=finer, in_specs=in_specs, out_specs=out_specs, check_vma=False)
```

time: 122 us -> 110 us (0.902)
  Pallas kernels: 59.4 us -> 52.4 us
  waiting for transfers between devices: 15.1 us -> 8.63 us
    pallas_call x2 -> x1, Pallas kernels: 35.5 us -> 28.2 us  [pair_call(): pl.pallas_call(functools.partial(pair_kernel, chans), in_specs=[smem] * 3...]
    ppermute x9 -> x6, waiting for transfers between devices: 11.3 us -> 4.8 us  [swap(): return lax.ppermute(array, axis, pairs)]
    ppermute x9 -> x6, starting transfers between devices: 14.5 us -> 8.95 us  [swap(): return lax.ppermute(array, axis, pairs)]
    ppermute x0 -> x3, starting transfers between devices: none -> 5.01 us  [body(): right_came.append(lax.ppermute(right_parts[q], 'row', pairs))]
    optimization_barrier x0 -> x1, local copies, waits for them, and re-layouts: none -> 2.36 us  [body(): across, ap, bt, bp = lax.optimization_barrier((across, ap, bt, bt.T))]
    convert_element_type x6 -> x4, other arithmetic: 3.24 us -> 3.86 us  [join(): return (keep.astype(F32) + came.astype(F32)).astype(dtype)]
    unnamed x26 -> x24, local copies, waits for them, and re-layouts: 8.94 us -> 8.37 us
  transfers between devices with their start and end apart: 13 -> 13, of which waited for: 6 -> 4; matrix products, arithmetic and copies ran while one was open for 12% -> 13% of each run, Pallas kernels for 28% -> 22%
where the time goes in v3:
time: 110 us; the launch traced here: 109 us
  Pallas kernels  52.4 us (48%)
  starting transfers between devices  28 us (25%)
  local copies, waits for them, and re-layouts  13.9 us (13%)
  waiting for transfers between devices  8.63 us (8%)
  other arithmetic  5.6 us (5%)
    pallas_call x1, Pallas kernels, pair_call(): pl.pallas_call(functools.partial(pair_kernel, chans), in_specs=[smem] * 3...  28.2 us
    pallas_call x1, Pallas kernels, weight_call(): pl.pallas_call(functools.partial(weight_kernel, chans), grid=(cols // her...  17.7 us
    all_to_all x1, starting transfers between devices, body(): lax.all_to_all(weight_part.reshape(128, -1, weight_part.shape[1]), EVERY,...  10.6 us
    ppermute x6, starting transfers between devices, swap(): return lax.ppermute(array, axis, pairs)  8.95 us
    unnamed x24, local copies, waits for them, and re-layouts  8.37 us
    ppermute x3, starting transfers between devices, body(): right_came.append(lax.ppermute(right_parts[q], 'row', pairs))  5.01 us
    ppermute x6, waiting for transfers between devices, swap(): return lax.ppermute(array, axis, pairs)  4.8 us
    convert_element_type x4, other arithmetic, join(): return (keep.astype(F32) + came.astype(F32)).astype(dtype)  3.86 us
  transfers between devices with their start and end apart: 13, of which 4 were waited for; matrix products, arithmetic and copies ran while one was open for 13% of the time, Pallas kernels for 22%

profile of v3, /device:TPU:0, one launch (start us, length us, event | category | flops | bytes accessed | tf_op | source)
XLA Modules:
  0.0 109.3 jit_solution(2351868404684313292)
XLA Ops:
  0.6 1.4 %copy.41 = bf16[32,64,128]{2,0,1:T(8,128)(2,1)S(1)} copy(bf16[32,64,128]{2,1,0:T(8,128)(2,1)} %param.7) | data formatting | bytes 1048576 | tf_op args[3]
  2.0 3.4 %collective-permute-start.1 = (bf16[64,32,128]{2,1,0:T(8,128)(2,1)S(1)}, bf16[64,32,128]{2,1,0:T(8,128)(2,1)S(1)}, u32[]{:S(2)}, u32[]{:S(2)}) collective-permute-start(bf16[64,32,128]{2,1,0:T(8,128)(2,1)S(1)} %bitcast.52), channel_id=1, source_target_pairs={{0,64},{32,96},{64,0},{96,32},{1,65},{33,97},{65,1},{97,33},{2,66}... | collective-permute-start | bytes 1572872 | tf_op jit(solution)/shard_map/ppermute | solution.py:224
  5.4 2.9 %copy.11 = bf16[64,32,448]{2,1,0:T(8,128)(2,1)S(1)} copy(bf16[64,32,448]{2,0,1:T(8,128)(2,1)} %bitcast.46) | data formatting | bytes 3670016 | tf_op jit(solution)/shard_map/transpose | solution.py:267
  8.3 5.2 %copy.40 = bf16[56,8,32,128]{3,1,2,0:T(8,128)(2,1)} copy(bf16[56,8,32,128]{3,2,1,0:T(8,128)(2,1)S(1)} %bitcast.43) | data formatting | bytes 7340032
  13.5 3.8 %collective-permute-done.1.g2 = bf16[64,32,128]{2,1,0:T(8,128)(2,1)S(1)} collective-permute-done((bf16[64,32,128]{2,1,0:T(8,128)(2,1)S(1)}, bf16[64,32,128]{2,1,0:T(8,128)(2,1)S(1)}, u32[]{:S(2)}, u32[]{:S(2)}) %collective-permute-start.1) | collective-permute-done | bytes 524320 | tf_op jit(solution)/shard_map/ppermute | solution.py:224
  17.3 0.8 pad_add_fusion
  18.1 2.4 %copy.12.bp_ref = bf16[448,2048]{1,0:T(8,128)(2,1)} copy(bf16[448,2048]{0,1:T(8,128)(2,1)S(1)} %bitcast.41) | data formatting | bytes 3670016 | tf_op jit(solution)/shard_map/optimization_barrier | solution.py:269
  20.4 28.2 %pair.1 = (bf16[4,224,512]{2,1,0:T(8,128)(2,1)}, bf16[4,224,512]{2,1,0:T(8,128)(2,1)}, bf16[4,224,512]{2,1,0:T(8,128)(2,1)}, bf16[4,224,512]{2,1,0:T(8,128)(2,1)...) custom-call(s32[1]{0:T(128)} %bitcast.me_ref, ...), custom_call_target="tpu_custom_call" | custom-call | flops 19327352832 | bytes 9175040 | tf_op jit(solution)/shard_map/pair/pallas_call | solution.py:101
  48.7 4.0 %collective-permute-start.5 = (bf16[112,2048]{1,0:T(8,128)(2,1)}, bf16[112,2048]{1,0:T(8,128)(2,1)S(1)}, u32[]{:S(2)}, u32[]{:S(2)}) collective-permute-start(bf16[112,2048]{1,0:T(8,128)(2,1)} %get-tuple-element.35), channel_id=1, source_target_pairs={{0,16},{8,24},{16,0},{24,8},{1,17},{9,25},{17,1},{25,9},{2,18},{10... | collective-permute-start | bytes 1376264 | tf_op jit(solution)/shard_map/ppermute | solution.py:280
  53.7 1.4 %collective-permute-start.3 = (bf16[4,224,512]{2,1,0:T(8,128)(2,1)}, bf16[4,224,512]{2,1,0:T(8,128)(2,1)S(1)}, u32[]{:S(2)}, u32[]{:S(2)}) collective-permute-start(bf16[4,224,512]{2,1,0:T(8,128)(2,1)} %get-tuple-element.32), channel_id=1, source_target_pairs={{0,2},{2,0},{4,6},{6,4},{1,3},{3,1},{5,7},{7,5},{8,10},{10,8},{12,... | collective-permute-start | bytes 2752520 | tf_op jit(solution)/shard_map/ppermute | solution.py:248
  55.1 2.1 %collective-permute-start.4 = (bf16[4,224,512]{2,1,0:T(8,128)(2,1)}, bf16[4,224,512]{2,1,0:T(8,128)(2,1)S(1)}, u32[]{:S(2)}, u32[]{:S(2)}) collective-permute-start(bf16[4,224,512]{2,1,0:T(8,128)(2,1)} %get-tuple-element.33), channel_id=1, source_target_pairs={{0,6},{2,4},{4,2},{6,0},{1,7},{3,5},{5,3},{7,1},{8,14},{10,12},{12... | collective-permute-start | bytes 2752520 | tf_op jit(solution)/shard_map/ppermute | solution.py:248
  57.3 17.7 %weight.1 = bf16[1024,128]{1,0:T(8,128)(2,1)} custom-call(s32[1]{0:T(128)} %bitcast.me_ref, bf16[64,32,128]{2,1,0:T(8,128)(2,1)} %bitcast.55, bf16[64,32,128]{2,1,0:T(8,128)(2,1)} %collective-permute-done.g1, bf16[64,32,128]{2,1,0:T(8,128)(2,1)} %copy-done.10, bf16[64,32,128]{2,1,0:T(8,128)(2,1)} %collective-permute-done.2.g3, bf16[2048,448]{1,0:T(8,128)(2,1)} %bitcast.42, ...), custom_call_target="tpu_custom_call" | custom-call | flops 11811160064 | bytes 5505024 | tf_op jit(solution)/shard_map/weight/pallas_call | solution.py:197
  75.0 1.1 %copy-done.2 = bf16[4,224,512]{2,1,0:T(8,128)(2,1)S(1)} copy-done((bf16[4,224,512]{2,1,0:T(8,128)(2,1)S(1)}, bf16[4,224,512]{2,1,0:T(8,128)(2,1)}, u32[]{:S(2)}) %copy-start.2) | copy-done | bytes 917528
  76.3 2.1 %collective-permute-done.4 = bf16[4,224,512]{2,1,0:T(8,128)(2,1)S(1)} collective-permute-done((bf16[4,224,512]{2,1,0:T(8,128)(2,1)}, bf16[4,224,512]{2,1,0:T(8,128)(2,1)S(1)}, u32[]{:S(2)}, u32[]{:S(2)}) %collective-permute-start.4) | collective-permute-done | bytes 917536 | tf_op jit(solution)/shard_map/ppermute | solution.py:248
  78.6 0.9 fusion
  79.5 1.7 %collective-permute-start.8 = (bf16[4,2,56,512]{3,2,0,1:T(8,128)(2,1)}, bf16[4,2,56,512]{3,2,0,1:T(8,128)(2,1)}, u32[]{:S(2)}, u32[]{:S(2)}) collective-permute-start(bf16[4,2,56,512]{3,2,0,1:T(8,128)(2,1)} %fusion), channel_id=1, source_target_pairs={{0,1},{1,0},{2,3},{3,2},{4,5},{5,4},{6,7},{7,6},{8,9},{9,8},{10,11... | collective-permute-start | bytes 1376264 | tf_op jit(solution)/shard_map/ppermute | solution.py:248
  81.6 10.6 %all-to-all-start = ((bf16[128,8,128]{2,1,0:T(8,128)(2,1)}), bf16[128,8,128]{2,1,0:T(8,128)(2,1)S(1)}, u32[]{:S(2)}, u32[]{:S(2)}) async-start(bf16[128,8,128]{2,1,0:T(8,128)(2,1)} %bitcast.19), calls=%async_computation | async-start | bytes 524288 | tf_op jit(solution)/shard_map/all_to_all | solution.py:302
  92.3 2.0 %fusion.2 = (bf16[4,56,512]{2,1,0:T(8,128)(2,1)S(1)}, f32[4,56,512]{2,1,0:T(8,128)}) fusion(f32[4,2,56,512]{3,2,0,1:T(8,128)S(1)} %add_bitcast_fusion.1, bf16[4,2,56,512]{3,2,0,1:T(8,128)(2,1)} %collective-permute-done.8), kind=kLoop, calls=%fused_computation.13 | loop fusion | flops 573440 | bytes 2064384 | tf_op jit(solution)/shard_map/convert_element_type | solution.py:252
  94.2 2.2 %collective-permute-start.9 = (bf16[4,56,512]{2,1,0:T(8,128)(2,1)S(1)}, bf16[4,56,512]{2,1,0:T(8,128)(2,1)S(1)}, u32[]{:S(2)}, u32[]{:S(2)}) collective-permute-start(bf16[4,56,512]{2,1,0:T(8,128)(2,1)S(1)} %get-tuple-element.55), channel_id=1, source_target_pairs={{0,6},{2,4},{4,2},{6,0},{1,7},{3,5},{5,3},{7,1},{8,14},{10,12},{12... | collective-permute-start | bytes 688136 | tf_op jit(solution)/shard_map/ppermute | solution.py:248
  96.4 0.9 fusion.3
  97.3 1.5 %collective-permute-start.11 = (bf16[4,56,512]{2,1,0:T(8,128)(2,1)S(1)}, bf16[4,56,512]{2,1,0:T(8,128)(2,1)S(1)}, u32[]{:S(2)}, u32[]{:S(2)}) collective-permute-start(bf16[4,56,512]{2,1,0:T(8,128)(2,1)S(1)} %get-tuple-element.53), channel_id=1, source_target_pairs={{0,1},{1,0},{2,3},{3,2},{4,5},{5,4},{6,7},{7,6},{8,9},{9,8},{10,11... | collective-permute-start | bytes 688136 | tf_op jit(solution)/shard_map/ppermute | solution.py:248
  98.8 3.3 %right_end.1 = f32[32,64,112]{2,1,0:T(8,128)} custom-call(bf16[112,2048]{1,0:T(8,128)(2,1)} %get-tuple-element.46.p0, bf16[112,2048]{1,0:T(8,128)(2,1)} %copy-done.5, bf16[112,2048]{1,0:T(8,128)(2,1)} %copy-done.6, bf16[112,2048]{1,0:T(8,128)(2,1)} %copy-done.7), custom_call_target="tpu_custom_call" | custom-call | flops 917504 | bytes 2752512 | tf_op jit(solution)/shard_map/right_end/pallas_call | solution.py:152
  102.6 2.1 %collective-permute-done.11.came_b = bf16[4,56,512]{2,1,0:T(8,128)(2,1)S(1)} collective-permute-done((bf16[4,56,512]{2,1,0:T(8,128)(2,1)S(1)}, bf16[4,56,512]{2,1,0:T(8,128)(2,1)S(1)}, u32[]{:S(2)}, u32[]{:S(2)}) %collective-permute-start.11) | collective-permute-done | bytes 229408 | tf_op jit(solution)/shard_map/ppermute | solution.py:248
  105.4 3.2 %left_end.1 = f32[56,32,128]{2,1,0:T(8,128)} custom-call(f32[4,56,512]{2,1,0:T(8,128)} %get-tuple-element.56.keep_a, bf16[4,56,512]{2,1,0:T(8,128)(2,1)} %copy-done.8, f32[4,56,512]{2,1,0:T(8,128)} %get-tuple-element.54.keep_b, bf16[4,56,512]{2,1,0:T(8,128)(2,1)} %copy-done.9), custom_call_target="tpu_custom_call" | custom-call | flops 458752 | bytes 1835008 | tf_op jit(solution)/shard_map/left_end/pallas_call | solution.py:131
  (45 shorter events, 3.8 us)
Async XLA Ops:
  2.0 6.3 %copy-start.4 = (bf16[32,64,128]{2,0,1:T(8,128)(2,1)}, bf16[32,64,128]{2,0,1:T(8,128)(2,1)S(1)}, u32[]{:S(2)}) copy-start(bf16[32,64,128]{2,0,1:T(8,128)(2,1)S(1)} %copy.41) | copy-start | bytes 1572868
  2.0 15.3 %collective-permute-start.1 = (bf16[64,32,128]{2,1,0:T(8,128)(2,1)S(1)}, bf16[64,32,128]{2,1,0:T(8,128)(2,1)S(1)}, u32[]{:S(2)}, u32[]{:S(2)}) collective-permute-start(bf16[64,32,128]{2,1,0:T(8,128)(2,1)S(1)} %bitcast.52), channel_id=1, source_target_pairs={{0,64},{32,96},{64,0},{96,32},{1,65},{33,97},{65,1},{97,33},{2,66}... | collective-permute-start | bytes 1572872 | tf_op jit(solution)/shard_map/ppermute | solution.py:224
  5.4 15.0 %collective-permute-start = (bf16[64,32,128]{2,1,0:T(8,128)(2,1)S(1)}, bf16[64,32,128]{2,1,0:T(8,128)(2,1)}, u32[]{:S(2)}, u32[]{:S(2)}) collective-permute-start(bf16[64,32,128]{2,1,0:T(8,128)(2,1)S(1)} %bitcast.53), channel_id=1, source_target_pairs={{0,32},{32,0},{64,96},{96,64},{1,33},{33,1},{65,97},{97,65},{2,34}... | collective-permute-start | bytes 1572872 | tf_op jit(solution)/shard_map/ppermute | solution.py:224
  5.4 2.9 %copy-start.1 = (bf16[448,32,128]{2,1,0:T(8,128)(2,1)S(1)}, bf16[448,32,128]{2,1,0:T(8,128)(2,1)}, u32[]{:S(2)}) copy-start(bf16[448,32,128]{2,1,0:T(8,128)(2,1)} %param.4) | copy-start | bytes 11010052
  8.3 9.8 %copy-start = (bf16[64,32,448]{2,1,0:T(8,128)(2,1)}, bf16[64,32,448]{2,1,0:T(8,128)(2,1)S(1)}, u32[]{:S(2)}) copy-start(bf16[64,32,448]{2,1,0:T(8,128)(2,1)S(1)} %copy.11) | copy-start | bytes 5505028
  17.3 3.1 %copy-start.10 = (bf16[64,32,128]{2,1,0:T(8,128)(2,1)}, bf16[64,32,128]{2,1,0:T(8,128)(2,1)S(1)}, u32[]{:S(2)}) copy-start(bf16[64,32,128]{2,1,0:T(8,128)(2,1)S(1)} %collective-permute-done.1.g2) | copy-start | bytes 1572868
  17.3 3.1 %collective-permute-start.2 = (bf16[64,32,128]{2,1,0:T(8,128)(2,1)S(1)}, bf16[64,32,128]{2,1,0:T(8,128)(2,1)}, u32[]{:S(2)}, u32[]{:S(2)}) collective-permute-start(bf16[64,32,128]{2,1,0:T(8,128)(2,1)S(1)} %collective-permute-done.1.g2), channel_id=1, source_target_pairs={{0,32},{32,0},{64,96},{96,64},{1,33},{33,1},{65,97},{97,65},{2,34}... | collective-permute-start | bytes 1572872 | tf_op jit(solution)/shard_map/ppermute | solution.py:224
  48.7 27.5 %collective-permute-start.5 = (bf16[112,2048]{1,0:T(8,128)(2,1)}, bf16[112,2048]{1,0:T(8,128)(2,1)S(1)}, u32[]{:S(2)}, u32[]{:S(2)}) collective-permute-start(bf16[112,2048]{1,0:T(8,128)(2,1)} %get-tuple-element.35), channel_id=1, source_target_pairs={{0,16},{8,24},{16,0},{24,8},{1,17},{9,25},{17,1},{25,9},{2,18},{10... | collective-permute-start | bytes 1376264 | tf_op jit(solution)/shard_map/ppermute | solution.py:280
  52.6 23.6 %collective-permute-start.6 = (bf16[112,2048]{1,0:T(8,128)(2,1)}, bf16[112,2048]{1,0:T(8,128)(2,1)S(1)}, u32[]{:S(2)}, u32[]{:S(2)}) collective-permute-start(bf16[112,2048]{1,0:T(8,128)(2,1)} %get-tuple-element.36), channel_id=1, source_target_pairs={{0,24},{8,16},{16,8},{24,0},{1,25},{9,17},{17,9},{25,1},{2,26},{10... | collective-permute-start | bytes 1376264 | tf_op jit(solution)/shard_map/ppermute | solution.py:280
  53.3 22.9 %collective-permute-start.7 = (bf16[112,2048]{1,0:T(8,128)(2,1)}, bf16[112,2048]{1,0:T(8,128)(2,1)S(1)}, u32[]{:S(2)}, u32[]{:S(2)}) collective-permute-start(bf16[112,2048]{1,0:T(8,128)(2,1)} %get-tuple-element.37), channel_id=1, source_target_pairs={{0,8},{8,0},{16,24},{24,16},{1,9},{9,1},{17,25},{25,17},{2,10},{10... | collective-permute-start | bytes 1376264 | tf_op jit(solution)/shard_map/ppermute | solution.py:280
  53.7 22.6 %collective-permute-start.3 = (bf16[4,224,512]{2,1,0:T(8,128)(2,1)}, bf16[4,224,512]{2,1,0:T(8,128)(2,1)S(1)}, u32[]{:S(2)}, u32[]{:S(2)}) collective-permute-start(bf16[4,224,512]{2,1,0:T(8,128)(2,1)} %get-tuple-element.32), channel_id=1, source_target_pairs={{0,2},{2,0},{4,6},{6,4},{1,3},{3,1},{5,7},{7,5},{8,10},{10,8},{12,... | collective-permute-start | bytes 2752520 | tf_op jit(solution)/shard_map/ppermute | solution.py:248
  55.1 19.8 %copy-start.3 = (bf16[4,224,512]{2,1,0:T(8,128)(2,1)S(1)}, bf16[4,224,512]{2,1,0:T(8,128)(2,1)}, u32[]{:S(2)}) copy-start(bf16[4,224,512]{2,1,0:T(8,128)(2,1)} %get-tuple-element.31) | copy-start | bytes 2752516
  55.1 23.3 %collective-permute-start.4 = (bf16[4,224,512]{2,1,0:T(8,128)(2,1)}, bf16[4,224,512]{2,1,0:T(8,128)(2,1)S(1)}, u32[]{:S(2)}, u32[]{:S(2)}) collective-permute-start(bf16[4,224,512]{2,1,0:T(8,128)(2,1)} %get-tuple-element.33), channel_id=1, source_target_pairs={{0,6},{2,4},{4,2},{6,0},{1,7},{3,5},{5,3},{7,1},{8,14},{10,12},{12... | collective-permute-start | bytes 2752520 | tf_op jit(solution)/shard_map/ppermute | solution.py:248
  74.9 1.2 %copy-start.2 = (bf16[4,224,512]{2,1,0:T(8,128)(2,1)S(1)}, bf16[4,224,512]{2,1,0:T(8,128)(2,1)}, u32[]{:S(2)}) copy-start(bf16[4,224,512]{2,1,0:T(8,128)(2,1)} %get-tuple-element.40) | copy-start | bytes 2752516
  76.2 3.3 %copy-start.5 = (bf16[112,2048]{1,0:T(8,128)(2,1)}, bf16[112,2048]{1,0:T(8,128)(2,1)S(1)}, u32[]{:S(2)}) copy-start(bf16[112,2048]{1,0:T(8,128)(2,1)S(1)} %collective-permute-done.5.p1) | copy-start | bytes 1376260
  76.2 3.2 %copy-start.6 = (bf16[112,2048]{1,0:T(8,128)(2,1)}, bf16[112,2048]{1,0:T(8,128)(2,1)S(1)}, u32[]{:S(2)}) copy-start(bf16[112,2048]{1,0:T(8,128)(2,1)S(1)} %collective-permute-done.6.p2) | copy-start | bytes 1376260
  76.2 3.2 %copy-start.7 = (bf16[112,2048]{1,0:T(8,128)(2,1)}, bf16[112,2048]{1,0:T(8,128)(2,1)S(1)}, u32[]{:S(2)}) copy-start(bf16[112,2048]{1,0:T(8,128)(2,1)S(1)} %collective-permute-done.7.p3) | copy-start | bytes 1376260
  79.5 12.8 %collective-permute-start.8 = (bf16[4,2,56,512]{3,2,0,1:T(8,128)(2,1)}, bf16[4,2,56,512]{3,2,0,1:T(8,128)(2,1)}, u32[]{:S(2)}, u32[]{:S(2)}) collective-permute-start(bf16[4,2,56,512]{3,2,0,1:T(8,128)(2,1)} %fusion), channel_id=1, source_target_pairs={{0,1},{1,0},{2,3},{3,2},{4,5},{5,4},{6,7},{7,6},{8,9},{9,8},{10,11... | collective-permute-start | bytes 1376264 | tf_op jit(solution)/shard_map/ppermute | solution.py:248
  81.3 15.1 %collective-permute-start.10 = (bf16[4,2,56,512]{3,2,0,1:T(8,128)(2,1)S(1)}, bf16[4,2,56,512]{3,2,0,1:T(8,128)(2,1)S(1)}, u32[]{:S(2)}, u32[]{:S(2)}) collective-permute-start(bf16[4,2,56,512]{3,2,0,1:T(8,128)(2,1)S(1)} %fusion.1), channel_id=1, source_target_pairs={{0,2},{2,0},{4,6},{6,4},{1,3},{3,1},{5,7},{7,5},{8,10},{10,8},{12,... | collective-permute-start | bytes 1376264 | tf_op jit(solution)/shard_map/ppermute | solution.py:248
  81.6 27.0 %all-to-all-start = ((bf16[128,8,128]{2,1,0:T(8,128)(2,1)}), bf16[128,8,128]{2,1,0:T(8,128)(2,1)S(1)}, u32[]{:S(2)}, u32[]{:S(2)}) async-start(bf16[128,8,128]{2,1,0:T(8,128)(2,1)} %bitcast.19), calls=%async_computation | async-start | bytes 524288 | tf_op jit(solution)/shard_map/all_to_all | solution.py:302
  94.2 8.4 %collective-permute-start.9 = (bf16[4,56,512]{2,1,0:T(8,128)(2,1)S(1)}, bf16[4,56,512]{2,1,0:T(8,128)(2,1)S(1)}, u32[]{:S(2)}, u32[]{:S(2)}) collective-permute-start(bf16[4,56,512]{2,1,0:T(8,128)(2,1)S(1)} %get-tuple-element.55), channel_id=1, source_target_pairs={{0,6},{2,4},{4,2},{6,0},{1,7},{3,5},{5,3},{7,1},{8,14},{10,12},{12... | collective-permute-start | bytes 688136 | tf_op jit(solution)/shard_map/ppermute | solution.py:248
  97.3 7.4 %collective-permute-start.11 = (bf16[4,56,512]{2,1,0:T(8,128)(2,1)S(1)}, bf16[4,56,512]{2,1,0:T(8,128)(2,1)S(1)}, u32[]{:S(2)}, u32[]{:S(2)}) collective-permute-start(bf16[4,56,512]{2,1,0:T(8,128)(2,1)S(1)} %get-tuple-element.53), channel_id=1, source_target_pairs={{0,1},{1,0},{2,3},{3,2},{4,5},{5,4},{6,7},{7,6},{8,9},{9,8},{10,11... | collective-permute-start | bytes 688136 | tf_op jit(solution)/shard_map/ppermute | solution.py:248
  102.6 2.1 %copy-start.8 = (bf16[4,56,512]{2,1,0:T(8,128)(2,1)}, bf16[4,56,512]{2,1,0:T(8,128)(2,1)S(1)}, u32[]{:S(2)}) copy-start(bf16[4,56,512]{2,1,0:T(8,128)(2,1)S(1)} %collective-permute-done.9.came_a) | copy-start | bytes 688132
  104.7 0.7 copy-start.9
